TPU v7x, 256 devices: a whole 4x4x8 slice. The times are simulated.
256 devices in a mesh: orb: 8 (over y_hi, x), pt: 32 (over y_lo, z, core).
Axes of the slice: x: 4, y: 4 (y_hi: 2, y_lo: 2; y = y_hi * 2 + y_lo), z: 8, core: 2. Of those that a mesh axis runs over, the one named last changes fastest.
Arguments:
- collocation: bfloat16 [2048, 49152], P('orb', 'pt'), may hold values from -0.8984375 to 0.8984375
- pair_tensor: bfloat16 [49152, 128], P('pt'), may hold values from -0.02734375 to 0.02734375
Outputs:
- fitted: float32 [4096, 128], P(('orb', 'pt'))
All inputs are finite; a program needn't handle non-finite values.
Results may differ from a plain program's by a relative error of at most 0.0034.
Values may be sent and summed in bfloat16 or wider, within the bound.
No kernel may reach another device: no remote copies, remote signals or barrier semaphores. Data moves between devices by JAX's collectives and lax.ppermute only.
A program may use at most 128 MiB of HBM per device.

v0:
```python
import jax
import jax.numpy as jnp
from jax import lax
from jax.sharding import PartitionSpec as P

PAN_DEV = 128


def on_device(collocation, pair_tensor):
    local_panel = collocation[:, :PAN_DEV]
    panel_cols = lax.all_gather(local_panel, "pt", axis=1, tiled=True)
    gram_block = lax.psum_scatter(
        lax.dot_general(
            panel_cols, collocation, (((0,), (0,)), ((), ())), preferred_element_type=jnp.float32
        ),
        "orb",
        scatter_dimension=0,
        tiled=True,
    )
    squared = (gram_block * gram_block).astype(jnp.bfloat16)
    partial_fit = jnp.dot(squared, pair_tensor, preferred_element_type=jnp.float32)
    return lax.psum_scatter(partial_fit, "pt", scatter_dimension=0, tiled=True)


def solution(mesh):
    return jax.shard_map(
        on_device,
        mesh=mesh,
        in_specs=(P("orb", "pt"), P("pt", None)),
        out_specs=P(("orb", "pt"), None),
        check_vma=False,
    )
```

profile of v0, /device:TPU:32, one launch (start us, length us, event | category | flops | bytes accessed | tf_op | source)
XLA Modules:
  0.0 479.3 jit_solution(17845330594539875762)
XLA Ops:
  6.5 0.0 copy-start
  6.5 0.0 all-gather.2.cloned.1.call-start
  6.5 1.5 slice.3
  8.1 0.0 all-gather.2.cloned.1.call-update
  8.1 0.0 reduce-scatter.3.cloned.1.call-start
  8.1 69.3 %all-gather.2.cloned.1.call-done = bf16[256,4096]{1,0:T(8,128)(2,1)} async-done(((bf16[256,128]{1,0:T(8,128)(2,1)}), bf16[256,4096]{1,0:T(8,128)(2,1)}) %all-gather.2.cloned.1.call-update) | async-done | bytes 2097168 | tf_op jit(solution)/shard_map/all_gather | solution.py:11
  77.5 13.5 %fusion.1 = f32[4096,1536]{1,0:T(8,128)} fusion(bf16[256,4096]{1,0:T(8,128)(2,1)} %all-gather.2.cloned.1.call-done, bf16[256,1536]{1,0:T(8,128)(2,1)} %param.2), kind=kOutput, calls=%fused_computation.2 | convolution fusion | flops 3221225472 | bytes 28049408 | tf_op jit(solution)/shard_map/dot_general | solution.py:13
  91.0 0.0 reduce-scatter.3.cloned.1.call-update
  91.0 0.0 reduce-scatter.5.cloned.1.call-start
  91.1 267.0 %reduce-scatter.3.cloned.1.call-done = f32[512,1536]{1,0:T(8,128)} async-done(((f32[4096,1536]{1,0:T(8,128)}), f32[512,1536]{1,0:T(8,128)}) %reduce-scatter.3.cloned.1.call-update) | async-done | bytes 3145744 | tf_op jit(solution)/shard_map/reduce_scatter | solution.py:12
  358.1 0.0 copy-done
  358.1 3.2 fusion
  361.3 0.0 reduce-scatter.5.cloned.1.call-update
  361.3 111.4 %reduce-scatter.5.cloned.1.call-done = f32[16,128]{1,0:T(8,128)} async-done(((f32[512,128]{1,0:T(8,128)}), f32[16,128]{1,0:T(8,128)}) %reduce-scatter.5.cloned.1.call-update) | async-done | bytes 8208 | tf_op jit(solution)/shard_map/reduce_scatter | solution.py:22
Async XLA Ops:
  6.5 351.6 %copy-start = (bf16[1536,128]{1,0:T(8,128)(2,1)S(1)}, bf16[1536,128]{1,0:T(8,128)(2,1)}, u32[]{:S(2)}) copy-start(bf16[1536,128]{1,0:T(8,128)(2,1)} %param.3) | copy-start | bytes 1179652
  6.5 70.9 %all-gather.2.cloned.1.call-start = ((), (), s32[]{:S(2)}) async-start(), calls=%async_computation.2 | async-start | bytes 2162688 | tf_op jit(solution)/shard_map/all_gather | solution.py:11
  8.1 350.0 %reduce-scatter.3.cloned.1.call-start = ((), (), s32[]{:S(2)}) async-start(), calls=%async_computation.3 | async-start | bytes 28311552 | tf_op jit(solution)/shard_map/reduce_scatter | solution.py:12
  91.0 381.7 %reduce-scatter.5.cloned.1.call-start = ((), (), s32[]{:S(2)}) async-start(), calls=%async_computation.4 | async-start | bytes 270336 | tf_op jit(solution)/shard_map/reduce_scatter | solution.py:22
Sparse Core Ops, SparseCore 0:
  9.1 68.2 all-gather.1
  91.1 266.9 reduce-scatter.2
  361.4 111.2 reduce-scatter.4
where the time goes:
time: 483 us; the launch traced here: 479 us
  waiting for transfers between devices  448 us (93%)
  matrix products  16.7 us (3%)
  between operations  13.1 us (3%)
    reduce_scatter x1, waiting for transfers between devices, on_device(): lax.psum_scatter(lax.dot_general(panel_cols, collocation, (((0,), (0,)),...  267 us
    reduce_scatter x1, waiting for transfers between devices, on_device(): return lax.psum_scatter(partial_fit, 'pt', scatter_dimension=0, tiled=True)  111 us
    all_gather x1, waiting for transfers between devices, on_device(): panel_cols = lax.all_gather(local_panel, 'pt', axis=1, tiled=True)  69.3 us
    dot_general x1, matrix products, on_device(): lax.dot_general(panel_cols, collocation, (((0,), (0,)), ((), ())), prefer...  13.5 us
  transfers between devices with their start and end apart: 3, of which 3 were waited for; matrix products, arithmetic and copies ran while one was open for 0% of the time, Pallas kernels for 0%

commit v1 on v0

v1 whole, which is shorter than its diff:
```python
import jax
import jax.numpy as jnp
import numpy as np
from jax import lax
from jax.sharding import Mesh, PartitionSpec as P

PAN_DEV = 128
AXES = ("yh", "x", "yl", "z", "c")
SIZES = (2, 4, 2, 8, 2)


def perm_of(move, only=lambda yh, x, yl, z, c: True):
    pairs = []
    for s in range(256):
        at = tuple(int(i) for i in np.unravel_index(s, SIZES))
        if only(*at):
            to = tuple(i % n for i, n in zip(move(*at), SIZES))
            pairs.append((s, int(np.ravel_multi_index(to, SIZES))))
    return pairs


def x_shift(d):
    return perm_of(lambda yh, x, yl, z, c: (yh, x + d, yl, z, c))


def z_shift(d):
    return perm_of(lambda yh, x, yl, z, c: (yh, x, yl, z + d, c))


CORE = perm_of(lambda yh, x, yl, z, c: (yh, x, yl, z, 1 - c))
Y_LO = perm_of(lambda yh, x, yl, z, c: (yh, x, 1 - yl, z, c))
Y_HI = perm_of(lambda yh, x, yl, z, c: (1 - yh, x, yl, z, c))
Y_BOTH = perm_of(lambda yh, x, yl, z, c: (1 - yh, x, 1 - yl, z, c))
TRADE = perm_of(lambda yh, x, yl, z, c: (1 - yh, x, yl, z, 1 - c), lambda yh, x, yl, z, c: c != yh)
SPREAD = perm_of(lambda yh, x, yl, z, c: (yh, z // 2, yl, 2 * x + z % 2, c))
SPREAD_CROSS = perm_of(lambda yh, x, yl, z, c: (yh, z // 2, yl, 2 * x + z % 2, 1 - c))


def send(a, perm):
    return lax.ppermute(a, AXES, perm)


def picker():
    m = np.zeros((2, 2, 4, 2, 16, 2, 4, 16), np.float32)
    for c in range(2):
        for src in range(2):
            for jj in range(4):
                for i in range(16):
                    m[c, src, jj, c, i, src, jj, i] = 1
    return m.reshape(2, 256, 128)


def on_device(collocation, pair_tensor):
    yh, x, yl, z, c = (lax.axis_index(a) for a in AXES)
    local_panel = collocation[:, :PAN_DEV]
    same, cross = send(local_panel, SPREAD), send(local_panel, SPREAD_CROSS)
    traded = send(collocation, TRADE)
    pair_cross = send(pair_tensor, CORE)

    pick = jnp.asarray(picker(), jnp.bfloat16)
    first = jnp.where(c == 0, same, cross)
    second = jnp.where(c == 0, cross, same)
    block = jnp.dot(
        jnp.concatenate([first, second], axis=1), pick[c], preferred_element_type=jnp.float32
    ).astype(jnp.bfloat16)

    ring = jnp.stack([block] + [send(block, z_shift(-d)) for d in range(1, 8)])
    ring = jnp.concatenate([ring, ring])
    ring = lax.dynamic_slice_in_dim(ring, lax.rem(2 * x - z + 8, 8), 8)
    slab = ring.reshape(4, 2, 256, 128).transpose(0, 2, 1, 3).reshape(1024, 256)
    lo, hi, both = send(slab, Y_LO), send(slab, Y_HI), send(slab, Y_BOTH)
    near = jnp.where(yl == 0, jnp.concatenate([slab, lo], 1), jnp.concatenate([lo, slab], 1))
    far = jnp.where(yl == 0, jnp.concatenate([hi, both], 1), jnp.concatenate([both, hi], 1))

    held = jnp.where(c == yh, collocation, traded)
    mine = jnp.concatenate([held] + [send(held, x_shift(-d)) for d in range(1, 4)])
    others = send(mine, CORE)

    def gram(panel, cols):
        return lax.dot_general(panel, cols, (((0,), (0,)), ((), ())), preferred_element_type=jnp.float32)

    on_near, on_far = jnp.where(c == yh, mine, others), jnp.where(c == yh, others, mine)
    gram_block = gram(jnp.concatenate([near, far]), jnp.concatenate([on_near, on_far]))
    squared = (gram_block * gram_block).astype(jnp.bfloat16)
    pair = jnp.where(c == yh, pair_tensor, pair_cross)
    part = jnp.dot(squared, pair, preferred_element_type=jnp.float32)
    parts = lax.all_to_all(part.reshape(32, 16, 128), ("yh", "yl", "z"), 0, 0)
    return parts.sum(0)


def solution(mesh):
    return jax.shard_map(
        on_device,
        mesh=Mesh(mesh.devices.reshape(SIZES), AXES),
        in_specs=(P(("yh", "x"), ("yl", "z", "c")), P(("yl", "z", "c"), None)),
        out_specs=P(AXES, None),
        check_vma=False,
    )
```

time: 483 us -> 138 us (0.29)
  waiting for transfers between devices: 448 us -> 48.1 us
  starting transfers between devices: 0.09 us -> 40.8 us
  blocking collectives: 0 us -> 19.2 us
  other arithmetic: 0 us -> 14 us
  between operations: 13.1 us -> 0.13 us
  matrix products: 16.7 us -> 9.35 us
    reduce_scatter x2 -> x0, waiting for transfers between devices: 378 us -> none  [the longest x1 267 us: on_device(): lax.psum_scatter(lax.dot_general(panel_cols, collocation, (((0,), (0,)),...]
    all_gather x1 -> x0, waiting for transfers between devices: 69.3 us -> none  [on_device(): panel_cols = lax.all_gather(local_panel, 'pt', axis=1, tiled=True)]
    ppermute x0 -> x18, waiting for transfers between devices: none -> 48.1 us  [send(): return lax.ppermute(a, AXES, perm)]
    ppermute x0 -> x18, starting transfers between devices: none -> 40.8 us  [send(): return lax.ppermute(a, AXES, perm)]
    all_to_all x0 -> x1, blocking collectives: none -> 19.2 us  [on_device(): parts = lax.all_to_all(part.reshape(32, 16, 128), ('yh', 'yl', 'z'), 0, 0)]
    select_n x0 -> x5, other arithmetic: none -> 11.6 us  [the longest x1 4.78 us: on_device(): jnp.where(c == yh, mine, others)]
    dot_general x2, matrix products: 16.7 us -> 9.35 us  [the longest x1 7.71 us: on_device(): part = jnp.dot(squared, pair, preferred_element_type=jnp.float32)]
  transfers between devices with their start and end apart: 3 -> 18, of which waited for: 3 -> 6; matrix products, arithmetic and copies ran while one was open for 0% -> 15% of each run, Pallas kernels for 0% -> 0%
where the time goes in v1:
time: 138 us; the launch traced here: 137 us
  waiting for transfers between devices  48.1 us (35%)
  starting transfers between devices  40.8 us (30%)
  blocking collectives  19.2 us (14%)
  other arithmetic  14 us (10%)
  matrix products  9.35 us (7%)
  local copies, waits for them, and re-layouts  5.57 us (4%)
    ppermute x18, waiting for transfers between devices, send(): return lax.ppermute(a, AXES, perm)  48.1 us
    ppermute x18, starting transfers between devices, send(): return lax.ppermute(a, AXES, perm)  40.8 us
    all_to_all x1, blocking collectives, on_device(): parts = lax.all_to_all(part.reshape(32, 16, 128), ('yh', 'yl', 'z'), 0, 0)  19.2 us
    dot_general x1, matrix products, on_device(): part = jnp.dot(squared, pair, preferred_element_type=jnp.float32)  7.71 us
    select_n x1, other arithmetic, on_device(): jnp.where(c == yh, mine, others)  4.78 us
    unnamed x17, local copies, waits for them, and re-layouts  4.13 us
    select_n x1, other arithmetic, on_device(): jnp.where(yl == 0, jnp.concatenate([slab, lo], 1), jnp.concatenate([lo, s...  2.82 us
  transfers between devices with their start and end apart: 18, of which 6 were waited for; matrix products, arithmetic and copies ran while one was open for 15% of the time, Pallas kernels for 0%

profile of v1, /device:TPU:32, one launch (start us, length us, event | category | flops | bytes accessed | tf_op | source)
XLA Modules:
  0.0 137.2 jit_solution(7586363262037077594)
XLA Ops:
  0.0 0.7 collective-permute-start.12
  0.7 0.8 slice.3
  1.6 0.7 collective-permute-start
  2.2 4.6 %collective-permute-start.1 = (bf16[256,128]{1,0:T(8,128)(2,1)S(1)}, bf16[256,128]{1,0:T(8,128)(2,1)S(1)}, u32[]{:S(2)}, u32[]{:S(2)}) collective-permute-start(bf16[256,128]{1,0:T(8,128)(2,1)S(1)} %slice.3), channel_id=1, source_target_pairs={{0,1},{1,0},{2,3},{3,2},{4,33},{5,32},{6,35},{7,34},{8,65},{9,64},... | collective-permute-start | bytes 196616 | tf_op jit(solution)/shard_map/ppermute | solution.py:40
  6.8 0.9 collective-permute-done.1
  7.7 1.6 %bitcast_dynamic-update-slice_fusion.14 = (bf16[16,256,128]{2,1,0:T(8,128)(2,1)}, bf16[256,128]{1,0:T(8,128)(2,1)S(1)}) fusion(bf16[2,256,128]{2,1,0:T(8,128)(2,1)} %constant.36.clone, s32[]{:T(128)S(6)} %select_n.62, bf16[256,128]{1,0:T(8,128)(2,1)S(1)} %get-tuple-element.8, bf16[256,128]{1,0:T(8,128)(2,1)S(1)} %get-tuple-element.7), kind=kOutput, calls=%fused_computation.37 | convolution fusion | flops 17072128 | bytes 327684 | tf_op jit(solution)/shard_map/dot_general | solution.py:63
  9.5 19.3 %collective-permute-start.3 = (bf16[256,128]{1,0:T(8,128)(2,1)S(1)}, bf16[256,128]{1,0:T(8,128)(2,1)S(1)}, u32[]{:S(2)}, u32[]{:S(2)}) collective-permute-start(bf16[256,128]{1,0:T(8,128)(2,1)S(1)} %get-tuple-element.10), channel_id=1, source_target_pairs={{0,12},{1,13},{2,14},{3,15},{4,0},{5,1},{6,2},{7,3},{8,4},{9,5},{1... | collective-permute-start | bytes 196616 | tf_op jit(solution)/shard_map/ppermute | solution.py:40
  28.8 1.0 collective-permute-start.5
  30.4 1.2 broadcast_select_fusion.2
  31.6 4.0 %collective-permute-start.15 = (bf16[256,1536]{1,0:T(8,128)(2,1)S(1)}, bf16[256,1536]{1,0:T(8,128)(2,1)S(1)}, u32[]{:S(2)}, u32[]{:S(2)}) collective-permute-start(bf16[256,1536]{1,0:T(8,128)(2,1)S(1)} %broadcast_select_fusion.2), channel_id=1, source_target_pairs={{0,32},{1,33},{2,34},{3,35},{4,36},{5,37},{6,38},{7,39},{8,40},{9,... | collective-permute-start | bytes 2359304 | tf_op jit(solution)/shard_map/ppermute | solution.py:40
  35.6 1.6 %collective-permute-start.14 = (bf16[256,1536]{1,0:T(8,128)(2,1)S(1)}, bf16[256,1536]{1,0:T(8,128)(2,1)S(1)}, u32[]{:S(2)}, u32[]{:S(2)}) collective-permute-start(bf16[256,1536]{1,0:T(8,128)(2,1)S(1)} %broadcast_select_fusion.2), channel_id=1, source_target_pairs={{0,64},{1,65},{2,66},{3,67},{4,68},{5,69},{6,70},{7,71},{8,72},{9,... | collective-permute-start | bytes 2359304 | tf_op jit(solution)/shard_map/ppermute | solution.py:40
  37.3 2.5 %collective-permute-start.13 = (bf16[256,1536]{1,0:T(8,128)(2,1)S(1)}, bf16[256,1536]{1,0:T(8,128)(2,1)S(1)}, u32[]{:S(2)}, u32[]{:S(2)}) collective-permute-start(bf16[256,1536]{1,0:T(8,128)(2,1)S(1)} %broadcast_select_fusion.2), channel_id=1, source_target_pairs={{0,96},{1,97},{2,98},{3,99},{4,100},{5,101},{6,102},{7,103},{8,104... | collective-permute-start | bytes 2359304 | tf_op jit(solution)/shard_map/ppermute | solution.py:40
  40.4 0.6 bitcast_dynamic-update-slice_fusion.8
  41.1 2.2 %collective-permute-start.7 = (bf16[256,128]{1,0:T(8,128)(2,1)S(1)}, bf16[256,128]{1,0:T(8,128)(2,1)S(1)}, u32[]{:S(2)}, u32[]{:S(2)}) collective-permute-start(bf16[256,128]{1,0:T(8,128)(2,1)S(1)} %get-tuple-element.10), channel_id=1, source_target_pairs={{0,4},{1,5},{2,6},{3,7},{4,8},{5,9},{6,10},{7,11},{8,12},{9,13},{1... | collective-permute-start | bytes 196616 | tf_op jit(solution)/shard_map/ppermute | solution.py:40
  43.3 0.6 bitcast_dynamic-update-slice_fusion.6
  43.9 5.2 %collective-permute-done.6 = bf16[256,128]{1,0:T(8,128)(2,1)S(1)} collective-permute-done((bf16[256,128]{1,0:T(8,128)(2,1)S(1)}, bf16[256,128]{1,0:T(8,128)(2,1)S(1)}, u32[]{:S(2)}, u32[]{:S(2)}) %collective-permute-start.6) | collective-permute-done | bytes 65568 | tf_op jit(solution)/shard_map/ppermute | solution.py:40
  49.1 0.6 bitcast_dynamic-update-slice_fusion.4
  49.7 3.8 %collective-permute-done.15 = bf16[256,1536]{1,0:T(8,128)(2,1)S(1)} collective-permute-done((bf16[256,1536]{1,0:T(8,128)(2,1)S(1)}, bf16[256,1536]{1,0:T(8,128)(2,1)S(1)}, u32[]{:S(2)}, u32[]{:S(2)}) %collective-permute-start.15) | collective-permute-done | bytes 786464 | tf_op jit(solution)/shard_map/ppermute | solution.py:40
  53.6 17.5 %collective-permute-done.14 = bf16[256,1536]{1,0:T(8,128)(2,1)S(1)} collective-permute-done((bf16[256,1536]{1,0:T(8,128)(2,1)S(1)}, bf16[256,1536]{1,0:T(8,128)(2,1)S(1)}, u32[]{:S(2)}, u32[]{:S(2)}) %collective-permute-start.14) | collective-permute-done | bytes 786464 | tf_op jit(solution)/shard_map/ppermute | solution.py:40
  71.1 1.8 %pad_maximum_fusion = bf16[1024,1536]{1,0:T(8,128)(2,1)} fusion(bf16[256,1536]{1,0:T(8,128)(2,1)S(1)} %collective-permute-done.15, bf16[256,1536]{1,0:T(8,128)(2,1)S(1)} %collective-permute-done.14, bf16[256,1536]{1,0:T(8,128)(2,1)S(1)} %collective-permute-done.13, bf16[256,1536]{1,0:T(8,128)(2,1)S(1)} %broadcast_select_fusion.2), kind=kLoop, calls=%fused_computation.5 | loop fusion | flops 12582912 | bytes 6291456 | tf_op jit(solution)/shard_map/concatenate | solution.py:76
  73.7 0.9 copy.7
  74.6 0.7 collective-permute-start.9
  75.3 1.3 collective-permute-start.11
  76.5 2.1 %collective-permute-start.10 = (bf16[1024,256]{1,0:T(8,128)(2,1)}, bf16[1024,256]{1,0:T(8,128)(2,1)}, u32[]{:S(2)}, u32[]{:S(2)}) collective-permute-start(bf16[1024,256]{1,0:T(8,128)(2,1)} %bitcast.37), channel_id=1, source_target_pairs={{0,128},{1,129},{2,130},{3,131},{4,132},{5,133},{6,134},{7,135},{8... | collective-permute-start | bytes 1572872 | tf_op jit(solution)/shard_map/ppermute | solution.py:40
  78.7 10.9 %collective-permute-done.9 = bf16[1024,256]{1,0:T(8,128)(2,1)} collective-permute-done((bf16[1024,256]{1,0:T(8,128)(2,1)}, bf16[1024,256]{1,0:T(8,128)(2,1)}, u32[]{:S(2)}, u32[]{:S(2)}) %collective-permute-start.9) | collective-permute-done | bytes 524320 | tf_op jit(solution)/shard_map/ppermute | solution.py:40
  89.6 2.8 %maximum_select_fusion = bf16[1024,512]{1,0:T(8,128)(2,1)} fusion(bf16[1024,256]{1,0:T(8,128)(2,1)} %collective-permute-done.9, bf16[1024,256]{1,0:T(8,128)(2,1)} %bitcast.37, pred[]{:T(512)S(6)} %eq.6), kind=kLoop, calls=%fused_computation.14 | loop fusion | flops 4718592 | bytes 2097153 | tf_op jit(solution)/shard_map/jit(_where)/select_n | solution.py:72
  92.4 9.6 %collective-permute-done.11 = bf16[1024,256]{1,0:T(8,128)(2,1)} collective-permute-done((bf16[1024,256]{1,0:T(8,128)(2,1)}, bf16[1024,256]{1,0:T(8,128)(2,1)}, u32[]{:S(2)}, u32[]{:S(2)}) %collective-permute-start.11) | collective-permute-done | bytes 524320 | tf_op jit(solution)/shard_map/ppermute | solution.py:40
  102.1 2.7 %maximum_select_fusion.1 = bf16[1024,512]{1,0:T(8,128)(2,1)} fusion(bf16[1024,256]{1,0:T(8,128)(2,1)} %collective-permute-done.11, bf16[1024,256]{1,0:T(8,128)(2,1)} %collective-permute-done.10, pred[]{:T(512)S(6)} %eq.6), kind=kLoop, calls=%fused_computation.15 | loop fusion | flops 4718592 | bytes 2097153 | tf_op jit(solution)/shard_map/jit(_where)/select_n | solution.py:73
  104.8 4.8 %broadcast_select_fusion.1 = (bf16[1024,1536]{1,0:T(8,128)(2,1)}, bf16[1024,1536]{1,0:T(8,128)(2,1)}) fusion(bf16[1024,1536]{1,0:T(8,128)(2,1)} %collective-permute-done.16, pred[]{:T(512)S(6)} %eq.16, bf16[256,1536]{1,0:T(8,128)(2,1)S(1)} %collective-permute-done.15, bf16[256,1536]{1,0:T(8,128)(2,1)S(1)} %collective-permute-done.14, ...), kind=kLoop, calls=%fused_computation.7 | loop fusion | flops 15728640 | bytes 12582913 | tf_op jit(solution)/shard_map/jit(_where)/select_n | solution.py:82
  109.6 7.7 %fusion.15 = f32[512,128]{1,0:T(8,128)S(1)} fusion(bf16[1024,1536]{1,0:T(8,128)(2,1)} %get-tuple-element.6, bf16[1024,1536]{1,0:T(8,128)(2,1)} %get-tuple-element.5, bf16[1024,512]{1,0:T(8,128)(2,1)} %maximum_select_fusion.1, bf16[1024,512]{1,0:T(8,128)(2,1)} %maximum_select_fusion, bf16[1536,128]{1,0:T(8,128)(2,1)} %param.4, ...), kind=kOutput, calls=%fused_computation.13 | convolution fusion | flops 3441098752 | bytes 9437185 | tf_op jit(solution)/shard_map/dot_general | solution.py:86
  117.3 19.2 %all_to_all.5 = f32[32,16,128]{2,1,0:T(8,128)S(1)} all-to-all(f32[32,16,128]{2,1,0:T(8,128)S(1)} %bitcast.40), channel_id=1, replica_groups=mesh['yh'=2,'x'=4,'yl'=2,'z'=8,'c'=2] {'yh','yl','z'}, dimensions={0} | all-to-all | bytes 524288 | tf_op jit(solution)/shard_map/all_to_all | solution.py:87
  136.6 0.6 reduce_sum.9
  (35 shorter events, 2.2 us)
Async XLA Ops:
  0.0 30.4 %collective-permute-start.12 = (bf16[256,1536]{1,0:T(8,128)(2,1)}, bf16[256,1536]{1,0:T(8,128)(2,1)S(1)}, u32[]{:S(2)}, u32[]{:S(2)}) collective-permute-start(bf16[256,1536]{1,0:T(8,128)(2,1)} %param.3), channel_id=1, source_target_pairs={{1,128},{3,130},{5,132},{7,134},{9,136},{11,138},{13,140},{15,142}... | collective-permute-start | bytes 2359304 | tf_op jit(solution)/shard_map/ppermute | solution.py:40
  1.6 5.3 %collective-permute-start = (bf16[256,128]{1,0:T(8,128)(2,1)S(1)}, bf16[256,128]{1,0:T(8,128)(2,1)S(1)}, u32[]{:S(2)}, u32[]{:S(2)}) collective-permute-start(bf16[256,128]{1,0:T(8,128)(2,1)S(1)} %slice.3), channel_id=1, source_target_pairs={{0,0},{1,1},{2,2},{3,3},{4,32},{5,33},{6,34},{7,35},{8,64},{9,65},... | collective-permute-start | bytes 196616 | tf_op jit(solution)/shard_map/ppermute | solution.py:40
  2.2 5.5 %collective-permute-start.1 = (bf16[256,128]{1,0:T(8,128)(2,1)S(1)}, bf16[256,128]{1,0:T(8,128)(2,1)S(1)}, u32[]{:S(2)}, u32[]{:S(2)}) collective-permute-start(bf16[256,128]{1,0:T(8,128)(2,1)S(1)} %slice.3), channel_id=1, source_target_pairs={{0,1},{1,0},{2,3},{3,2},{4,33},{5,32},{6,35},{7,34},{8,65},{9,64},... | collective-permute-start | bytes 196616 | tf_op jit(solution)/shard_map/ppermute | solution.py:40
  9.4 20.4 %collective-permute-start.2 = (bf16[256,128]{1,0:T(8,128)(2,1)S(1)}, bf16[256,128]{1,0:T(8,128)(2,1)S(1)}, u32[]{:S(2)}, u32[]{:S(2)}) collective-permute-start(bf16[256,128]{1,0:T(8,128)(2,1)S(1)} %get-tuple-element.10), channel_id=1, source_target_pairs={{0,14},{1,15},{2,0},{3,1},{4,2},{5,3},{6,4},{7,5},{8,6},{9,7},{10,... | collective-permute-start | bytes 196616 | tf_op jit(solution)/shard_map/ppermute | solution.py:40
  9.5 27.8 %collective-permute-start.3 = (bf16[256,128]{1,0:T(8,128)(2,1)S(1)}, bf16[256,128]{1,0:T(8,128)(2,1)S(1)}, u32[]{:S(2)}, u32[]{:S(2)}) collective-permute-start(bf16[256,128]{1,0:T(8,128)(2,1)S(1)} %get-tuple-element.10), channel_id=1, source_target_pairs={{0,12},{1,13},{2,14},{3,15},{4,0},{5,1},{6,2},{7,3},{8,4},{9,5},{1... | collective-permute-start | bytes 196616 | tf_op jit(solution)/shard_map/ppermute | solution.py:40
  28.8 11.7 %collective-permute-start.4 = (bf16[256,128]{1,0:T(8,128)(2,1)S(1)}, bf16[256,128]{1,0:T(8,128)(2,1)S(1)}, u32[]{:S(2)}, u32[]{:S(2)}) collective-permute-start(bf16[256,128]{1,0:T(8,128)(2,1)S(1)} %get-tuple-element.10), channel_id=1, source_target_pairs={{0,10},{1,11},{2,12},{3,13},{4,14},{5,15},{6,0},{7,1},{8,2},{9,3},... | collective-permute-start | bytes 196616 | tf_op jit(solution)/shard_map/ppermute | solution.py:40
  28.8 12.3 %collective-permute-start.5 = (bf16[256,128]{1,0:T(8,128)(2,1)S(1)}, bf16[256,128]{1,0:T(8,128)(2,1)S(1)}, u32[]{:S(2)}, u32[]{:S(2)}) collective-permute-start(bf16[256,128]{1,0:T(8,128)(2,1)S(1)} %get-tuple-element.10), channel_id=1, source_target_pairs={{0,8},{1,9},{2,10},{3,11},{4,12},{5,13},{6,14},{7,15},{8,0},{9,1},... | collective-permute-start | bytes 196616 | tf_op jit(solution)/shard_map/ppermute | solution.py:40
  31.6 22.0 %collective-permute-start.15 = (bf16[256,1536]{1,0:T(8,128)(2,1)S(1)}, bf16[256,1536]{1,0:T(8,128)(2,1)S(1)}, u32[]{:S(2)}, u32[]{:S(2)}) collective-permute-start(bf16[256,1536]{1,0:T(8,128)(2,1)S(1)} %broadcast_select_fusion.2), channel_id=1, source_target_pairs={{0,32},{1,33},{2,34},{3,35},{4,36},{5,37},{6,38},{7,39},{8,40},{9,... | collective-permute-start | bytes 2359304 | tf_op jit(solution)/shard_map/ppermute | solution.py:40
  35.6 35.4 %collective-permute-start.14 = (bf16[256,1536]{1,0:T(8,128)(2,1)S(1)}, bf16[256,1536]{1,0:T(8,128)(2,1)S(1)}, u32[]{:S(2)}, u32[]{:S(2)}) collective-permute-start(bf16[256,1536]{1,0:T(8,128)(2,1)S(1)} %broadcast_select_fusion.2), channel_id=1, source_target_pairs={{0,64},{1,65},{2,66},{3,67},{4,68},{5,69},{6,70},{7,71},{8,72},{9,... | collective-permute-start | bytes 2359304 | tf_op jit(solution)/shard_map/ppermute | solution.py:40
  37.3 33.8 %collective-permute-start.13 = (bf16[256,1536]{1,0:T(8,128)(2,1)S(1)}, bf16[256,1536]{1,0:T(8,128)(2,1)S(1)}, u32[]{:S(2)}, u32[]{:S(2)}) collective-permute-start(bf16[256,1536]{1,0:T(8,128)(2,1)S(1)} %broadcast_select_fusion.2), channel_id=1, source_target_pairs={{0,96},{1,97},{2,98},{3,99},{4,100},{5,101},{6,102},{7,103},{8,104... | collective-permute-start | bytes 2359304 | tf_op jit(solution)/shard_map/ppermute | solution.py:40
  40.4 8.7 %collective-permute-start.6 = (bf16[256,128]{1,0:T(8,128)(2,1)S(1)}, bf16[256,128]{1,0:T(8,128)(2,1)S(1)}, u32[]{:S(2)}, u32[]{:S(2)}) collective-permute-start(bf16[256,128]{1,0:T(8,128)(2,1)S(1)} %get-tuple-element.10), channel_id=1, source_target_pairs={{0,6},{1,7},{2,8},{3,9},{4,10},{5,11},{6,12},{7,13},{8,14},{9,15},... | collective-permute-start | bytes 196616 | tf_op jit(solution)/shard_map/ppermute | solution.py:40
  41.1 31.8 %collective-permute-start.7 = (bf16[256,128]{1,0:T(8,128)(2,1)S(1)}, bf16[256,128]{1,0:T(8,128)(2,1)S(1)}, u32[]{:S(2)}, u32[]{:S(2)}) collective-permute-start(bf16[256,128]{1,0:T(8,128)(2,1)S(1)} %get-tuple-element.10), channel_id=1, source_target_pairs={{0,4},{1,5},{2,6},{3,7},{4,8},{5,9},{6,10},{7,11},{8,12},{9,13},{1... | collective-permute-start | bytes 196616 | tf_op jit(solution)/shard_map/ppermute | solution.py:40
  49.1 23.8 %collective-permute-start.8 = (bf16[256,128]{1,0:T(8,128)(2,1)S(1)}, bf16[256,128]{1,0:T(8,128)(2,1)S(1)}, u32[]{:S(2)}, u32[]{:S(2)}) collective-permute-start(bf16[256,128]{1,0:T(8,128)(2,1)S(1)} %get-tuple-element.10), channel_id=1, source_target_pairs={{0,2},{1,3},{2,4},{3,5},{4,6},{5,7},{6,8},{7,9},{8,10},{9,11},{10,... | collective-permute-start | bytes 196616 | tf_op jit(solution)/shard_map/ppermute | solution.py:40
  49.7 23.2 %copy-start = (bf16[16,256,128]{2,1,0:T(8,128)(2,1)S(1)}, bf16[16,256,128]{2,1,0:T(8,128)(2,1)}, u32[]{:S(2)}) copy-start(bf16[16,256,128]{2,1,0:T(8,128)(2,1)} %bitcast_dynamic-update-slice_fusion.4) | copy-start | bytes 3145732
  72.9 31.9 %collective-permute-start.16 = (bf16[1024,1536]{1,0:T(8,128)(2,1)}, bf16[1024,1536]{1,0:T(8,128)(2,1)}, u32[]{:S(2)}, u32[]{:S(2)}) collective-permute-start(bf16[1024,1536]{1,0:T(8,128)(2,1)} %pad_maximum_fusion), channel_id=1, source_target_pairs={{0,1},{1,0},{2,3},{3,2},{4,5},{5,4},{6,7},{7,6},{8,9},{9,8},{10,11... | collective-permute-start | bytes 9437192 | tf_op jit(solution)/shard_map/ppermute | solution.py:40
  74.6 15.0 %collective-permute-start.9 = (bf16[1024,256]{1,0:T(8,128)(2,1)}, bf16[1024,256]{1,0:T(8,128)(2,1)}, u32[]{:S(2)}, u32[]{:S(2)}) collective-permute-start(bf16[1024,256]{1,0:T(8,128)(2,1)} %bitcast.37), channel_id=1, source_target_pairs={{0,16},{1,17},{2,18},{3,19},{4,20},{5,21},{6,22},{7,23},{8,24},{9,... | collective-permute-start | bytes 1572872 | tf_op jit(solution)/shard_map/ppermute | solution.py:40
  75.3 26.8 %collective-permute-start.11 = (bf16[1024,256]{1,0:T(8,128)(2,1)}, bf16[1024,256]{1,0:T(8,128)(2,1)}, u32[]{:S(2)}, u32[]{:S(2)}) collective-permute-start(bf16[1024,256]{1,0:T(8,128)(2,1)} %bitcast.37), channel_id=1, source_target_pairs={{0,144},{1,145},{2,146},{3,147},{4,148},{5,149},{6,150},{7,151},{8... | collective-permute-start | bytes 1572872 | tf_op jit(solution)/shard_map/ppermute | solution.py:40
  76.5 25.5 %collective-permute-start.10 = (bf16[1024,256]{1,0:T(8,128)(2,1)}, bf16[1024,256]{1,0:T(8,128)(2,1)}, u32[]{:S(2)}, u32[]{:S(2)}) collective-permute-start(bf16[1024,256]{1,0:T(8,128)(2,1)} %bitcast.37), channel_id=1, source_target_pairs={{0,128},{1,129},{2,130},{3,131},{4,132},{5,133},{6,134},{7,135},{8... | collective-permute-start | bytes 1572872 | tf_op jit(solution)/shard_map/ppermute | solution.py:40
  78.7 30.9 %collective-permute-start.17 = (bf16[1536,128]{1,0:T(8,128)(2,1)}, bf16[1536,128]{1,0:T(8,128)(2,1)S(1)}, u32[]{:S(2)}, u32[]{:S(2)}) collective-permute-start(bf16[1536,128]{1,0:T(8,128)(2,1)} %param.4), channel_id=1, source_target_pairs={{0,1},{1,0},{2,3},{3,2},{4,5},{5,4},{6,7},{7,6},{8,9},{9,8},{10,11... | collective-permute-start | bytes 1179656 | tf_op jit(solution)/shard_map/ppermute | solution.py:40

commit v2 on v0

v2 whole, which is shorter than its diff:
```python
import jax
import jax.numpy as jnp
import numpy as np
from jax import lax
from jax.experimental import pallas as pl
from jax.experimental.pallas import tpu as pltpu
from jax.sharding import Mesh, PartitionSpec as P

PAN_DEV = 128
AXES = ("yh", "x", "yl", "z", "c")
SIZES = (2, 4, 2, 8, 2)
TILE = 512


def perm_of(move, only=lambda yh, c: True):
    pairs = []
    for s in range(256):
        yh, x, yl, z, c = (int(i) for i in np.unravel_index(s, SIZES))
        if only(yh, c):
            x, y, z, c = move(x, 2 * yh + yl, z, c)
            y = y % 4
            pairs.append((s, int(np.ravel_multi_index((y // 2, x % 4, y % 2, z % 8, c), SIZES))))
    return pairs


def is_own(y, c):
    return c == y // 2


def own(yh, c):
    return c == yh


CORE = perm_of(lambda x, y, z, c: (x, y, z, 1 - c))
SPREAD = perm_of(lambda x, y, z, c: (z // 2, y, 2 * x + z % 2, c))
TRADE = perm_of(lambda x, y, z, c: (x, y, z, c) if is_own(y, c) else (x, y + 2, z, 1 - c))


def x_step(d):
    return perm_of(lambda x, y, z, c: (x + d if c == 0 else x - d, y, z, c))


def y_step(d):
    return perm_of(lambda x, y, z, c: (x, y + d if c == 0 else y - d, z, c))


def send(a, perm):
    return lax.ppermute(a, AXES, perm)


def picker():
    m = np.zeros((2, 2, 4, 2, 16, 2, 4, 16), np.float32)
    for c in range(2):
        for s in range(2):
            for j in range(4):
                for i in range(16):
                    m[c, s, j, c, i, c ^ s, j, i] = 1
    return m.reshape(2, 256, 128)


def tile_kernel(h0, h1, h2, h3, g0, g1, g2, g3, pair, cspair, y0, y1, y2, y3, out, blocks):
    yh, x, yl, c = (lax.axis_index(a) for a in ("yh", "x", "yl", "c"))
    side = 2 * c - 1
    for dy, ref in ((0, y0), (side, y1), (-side, y2), (2, y3)):
        blocks[lax.rem(2 * yh + yl + dy + 4, 4)] = ref[...]
    out[...] = jnp.zeros_like(out)

    @pl.loop(0, h0.shape[1] // TILE)
    def _(t):
        at = pl.ds(pl.multiple_of(t * TILE, TILE), TILE)
        gram = jnp.zeros((512, TILE), jnp.float32)
        for half, dx, cols in (
            (c, 0, h0), (c, side, h1), (c, -side, h2), (c, 2, h3),
            (1 - c, 0, g0), (1 - c, -side, g1), (1 - c, side, g2), (1 - c, 2, g3),
        ):
            rows = blocks[pl.ds(2 * half, 2), pl.ds(2 * lax.rem(x + dx + 4, 4), 2)].reshape(512, 256)
            gram += jnp.dot(rows, cols[:, at], preferred_element_type=jnp.float32)
        weights = jnp.where(c == yh, pair[at, :], cspair[at, :])
        out[...] += jnp.dot((gram * gram).astype(jnp.bfloat16), weights, preferred_element_type=jnp.float32)


def tile_product(*operands):
    return pl.pallas_call(
        tile_kernel,
        out_shape=jax.ShapeDtypeStruct((512, 128), jnp.float32),
        in_specs=[pl.BlockSpec(memory_space=pltpu.VMEM)] * len(operands),
        out_specs=pl.BlockSpec(memory_space=pltpu.VMEM),
        scratch_shapes=[pltpu.VMEM((4, 8, 128, 256), jnp.bfloat16)],
        compiler_params=pltpu.CompilerParams(vmem_limit_bytes=24 * 2**20),
        cost_estimate=pl.CostEstimate(flops=3_400_000_000, bytes_accessed=9_000_000, transcendentals=0),
    )(*operands)


def on_device(collocation, pair_tensor):
    c = lax.axis_index("c")

    h0 = send(collocation, TRADE)
    local_panel = send(collocation[:, :PAN_DEV], SPREAD)
    cspair = send(pair_tensor, CORE)

    both = jnp.concatenate([local_panel, send(local_panel, CORE)], axis=1)
    pick = lax.dynamic_index_in_dim(jnp.asarray(picker(), jnp.bfloat16), c, keepdims=False)
    block = lax.dot_general(
        pick, both, (((0,), (1,)), ((), ())), preferred_element_type=jnp.float32
    ).astype(jnp.bfloat16)
    block, h0 = lax.optimization_barrier((block, h0))
    ring = lax.all_to_all(jnp.broadcast_to(block[None], (8, 128, 256)), "z", 0, 0)

    h1, h2 = send(h0, x_step(1)), send(h0, x_step(-1))
    h = [h0, h1, h2, send(h1, x_step(1))]
    y1, y2 = send(ring, y_step(1)), send(ring, y_step(-1))
    g = [send(a, CORE) for a in h]
    part = tile_product(*h, *g, pair_tensor, cspair, ring, y1, y2, send(y1, y_step(1)))
    parts = lax.all_to_all(part.reshape(32, 16, 128), ("yh", "yl", "z"), 0, 0)
    return parts.sum(0)


def solution(mesh):
    return jax.shard_map(
        on_device,
        mesh=Mesh(mesh.devices.reshape(SIZES), AXES),
        in_specs=(P(("yh", "x"), ("yl", "z", "c")), P(("yl", "z", "c"), None)),
        out_specs=P(AXES, None),
        check_vma=False,
    )
```

time: 483 us -> 94.7 us (0.20)
  waiting for transfers between devices: 448 us -> 32.1 us
  starting transfers between devices: 0.09 us -> 32.6 us
  blocking collectives: 0 us -> 20.4 us
  matrix products: 16.7 us -> 0.2 us
  between operations: 13.1 us -> 0.05 us
  Pallas kernels: 0 us -> 5.79 us
    reduce_scatter x2 -> x0, waiting for transfers between devices: 378 us -> none  [the longest x1 267 us: on_device(): lax.psum_scatter(lax.dot_general(panel_cols, collocation, (((0,), (0,)),...]
    all_gather x1 -> x0, waiting for transfers between devices: 69.3 us -> none  [on_device(): panel_cols = lax.all_gather(local_panel, 'pt', axis=1, tiled=True)]
    all_to_all x0 -> x1, blocking collectives: none -> 20.4 us  [on_device(): parts = lax.all_to_all(part.reshape(32, 16, 128), ('yh', 'yl', 'z'), 0, 0)]
    ppermute x0 -> x14, starting transfers between devices: none -> 20.3 us  [send(): return lax.ppermute(a, AXES, perm)]
    ppermute x0 -> x14, waiting for transfers between devices: none -> 19.6 us  [send(): return lax.ppermute(a, AXES, perm)]
    dot_general x2 -> x1, matrix products: 16.7 us -> 0.2 us  [on_device(): lax.dot_general(pick, both, (((0,), (1,)), ((), ())), preferred_element_t...]
    all_to_all x0 -> x1, waiting for transfers between devices: none -> 12.5 us  [on_device(): lax.all_to_all(jnp.broadcast_to(block[None], (8, 128, 256)), 'z', 0, 0)]
    all_to_all x0 -> x1, starting transfers between devices: none -> 12.3 us  [on_device(): lax.all_to_all(jnp.broadcast_to(block[None], (8, 128, 256)), 'z', 0, 0)]
  transfers between devices with their start and end apart: 3 -> 15, of which waited for: 3 -> 6; matrix products, arithmetic and copies ran while one was open for 0% -> 2% of each run, Pallas kernels for 0% -> 0%
where the time goes in v2:
time: 94.7 us; the launch traced here: 93.4 us
  starting transfers between devices  32.6 us (34%)
  waiting for transfers between devices  32.1 us (34%)
  blocking collectives  20.4 us (22%)
  Pallas kernels  5.79 us (6%)
  local copies, waits for them, and re-layouts  1.7 us (2%)
    all_to_all x1, blocking collectives, on_device(): parts = lax.all_to_all(part.reshape(32, 16, 128), ('yh', 'yl', 'z'), 0, 0)  20.4 us
    ppermute x14, starting transfers between devices, send(): return lax.ppermute(a, AXES, perm)  20.3 us
    ppermute x14, waiting for transfers between devices, send(): return lax.ppermute(a, AXES, perm)  19.6 us
    all_to_all x1, waiting for transfers between devices, on_device(): lax.all_to_all(jnp.broadcast_to(block[None], (8, 128, 256)), 'z', 0, 0)  12.5 us
    all_to_all x1, starting transfers between devices, on_device(): lax.all_to_all(jnp.broadcast_to(block[None], (8, 128, 256)), 'z', 0, 0)  12.3 us
    pallas_call x1, Pallas kernels, tile_product(): pl.pallas_call(tile_kernel, out_shape=jax.ShapeDtypeStruct((512, 128), jn...  5.79 us
  transfers between devices with their start and end apart: 15, of which 6 were waited for; matrix products, arithmetic and copies ran while one was open for 2% of the time, Pallas kernels for 0%

profile of v2, /device:TPU:32, one launch (start us, length us, event | category | flops | bytes accessed | tf_op | source)
XLA Modules:
  0.0 93.4 jit_solution(224211873524319752)
XLA Ops:
  0.0 1.9 %collective-permute-start.2 = (bf16[256,1536]{1,0:T(8,128)(2,1)}, bf16[256,1536]{1,0:T(8,128)(2,1)S(1)}, u32[]{:S(2)}, u32[]{:S(2)}) collective-permute-start(bf16[256,1536]{1,0:T(8,128)(2,1)} %param.3), channel_id=1, source_target_pairs={{0,0},{1,128},{2,2},{3,130},{4,4},{5,132},{6,6},{7,134},{8,8},{9,1... | collective-permute-start | bytes 2359304 | tf_op jit(solution)/shard_map/ppermute | solution.py:48
  1.9 0.8 slice.3
  2.8 0.7 collective-permute-start
  3.4 0.0 collective-permute-done
  3.4 3.5 %collective-permute-start.1 = (bf16[256,128]{1,0:T(8,128)(2,1)S(1)}, bf16[256,128]{1,0:T(8,128)(2,1)S(1)}, u32[]{:S(2)}, u32[]{:S(2)}) collective-permute-start(bf16[256,128]{1,0:T(8,128)(2,1)S(1)} %collective-permute-done), channel_id=1, source_target_pairs={{0,1},{1,0},{2,3},{3,2},{4,5},{5,4},{6,7},{7,6},{8,9},{9,8},{10,11... | collective-permute-start | bytes 196616 | tf_op jit(solution)/shard_map/ppermute | solution.py:48
  7.0 0.9 collective-permute-done.1
  7.9 0.2 convolution_convert_fusion
  8.1 0.0 collective-permute-done.2.h0
  8.1 7.6 %collective-permute-start.3 = (bf16[256,1536]{1,0:T(8,128)(2,1)S(1)}, bf16[256,1536]{1,0:T(8,128)(2,1)S(1)}, u32[]{:S(2)}, u32[]{:S(2)}) collective-permute-start(bf16[256,1536]{1,0:T(8,128)(2,1)S(1)} %collective-permute-done.2.h0), channel_id=1, source_target_pairs={{0,32},{1,97},{2,34},{3,99},{4,36},{5,101},{6,38},{7,103},{8,40},{... | collective-permute-start | bytes 2359304 | tf_op jit(solution)/shard_map/ppermute | solution.py:48
  15.7 0.8 broadcast_in_dim.2
  16.5 12.3 %all-to-all-start = ((bf16[8,128,256]{2,1,0:T(8,128)(2,1)}), bf16[8,128,256]{2,1,0:T(8,128)(2,1)S(1)}, u32[]{:S(2)}, u32[]{:S(2)}) async-start(bf16[8,128,256]{2,1,0:T(8,128)(2,1)} %broadcast_in_dim.2), calls=%async_computation | async-start | bytes 1048576 | tf_op jit(solution)/shard_map/all_to_all | solution.py:107
  28.9 2.6 %collective-permute-start.4 = (bf16[256,1536]{1,0:T(8,128)(2,1)S(1)}, bf16[256,1536]{1,0:T(8,128)(2,1)S(1)}, u32[]{:S(2)}, u32[]{:S(2)}) collective-permute-start(bf16[256,1536]{1,0:T(8,128)(2,1)S(1)} %collective-permute-done.2.h0), channel_id=1, source_target_pairs={{0,96},{1,33},{2,98},{3,35},{4,100},{5,37},{6,102},{7,39},{8,104},... | collective-permute-start | bytes 2359304 | tf_op jit(solution)/shard_map/ppermute | solution.py:48
  31.5 0.0 collective-permute-done.3.h1
  31.5 0.3 collective-permute-start.5
  31.8 0.2 collective-permute-start.6
  32.0 0.3 collective-permute-start.10
  32.3 12.5 %all-to-all-done.y0 = bf16[8,128,256]{2,1,0:T(8,128)(2,1)S(1)} async-done(((bf16[8,128,256]{2,1,0:T(8,128)(2,1)}), bf16[8,128,256]{2,1,0:T(8,128)(2,1)S(1)}, u32[]{:S(2)}, u32[]{:S(2)}) %all-to-all-start) | async-done | bytes 524320 | tf_op jit(solution)/shard_map/all_to_all | solution.py:107
  44.8 0.7 collective-permute-start.11
  45.5 3.8 %collective-permute-done.4.h2 = bf16[256,1536]{1,0:T(8,128)(2,1)S(1)} collective-permute-done((bf16[256,1536]{1,0:T(8,128)(2,1)S(1)}, bf16[256,1536]{1,0:T(8,128)(2,1)S(1)}, u32[]{:S(2)}, u32[]{:S(2)}) %collective-permute-start.4) | collective-permute-done | bytes 786464 | tf_op jit(solution)/shard_map/ppermute | solution.py:48
  49.3 0.0 collective-permute-start.8
  49.3 0.0 collective-permute-done.10.cspair
  49.3 0.5 collective-permute-start.7
  49.8 0.1 collective-permute-start.9
  49.9 1.9 %collective-permute-start.12 = (bf16[8,128,256]{2,1,0:T(8,128)(2,1)S(1)}, bf16[8,128,256]{2,1,0:T(8,128)(2,1)S(1)}, u32[]{:S(2)}, u32[]{:S(2)}) collective-permute-start(bf16[8,128,256]{2,1,0:T(8,128)(2,1)S(1)} %all-to-all-done.y0), channel_id=1, source_target_pairs={{0,144},{1,17},{2,146},{3,19},{4,148},{5,21},{6,150},{7,23},{8,152... | collective-permute-start | bytes 1572872 | tf_op jit(solution)/shard_map/ppermute | solution.py:48
  51.8 4.5 %collective-permute-done.11.y1 = bf16[8,128,256]{2,1,0:T(8,128)(2,1)S(1)} collective-permute-done((bf16[8,128,256]{2,1,0:T(8,128)(2,1)S(1)}, bf16[8,128,256]{2,1,0:T(8,128)(2,1)S(1)}, u32[]{:S(2)}, u32[]{:S(2)}) %collective-permute-start.11) | collective-permute-done | bytes 524320 | tf_op jit(solution)/shard_map/ppermute | solution.py:48
  56.3 8.0 %collective-permute-done.12.y2 = bf16[8,128,256]{2,1,0:T(8,128)(2,1)S(1)} collective-permute-done((bf16[8,128,256]{2,1,0:T(8,128)(2,1)S(1)}, bf16[8,128,256]{2,1,0:T(8,128)(2,1)S(1)}, u32[]{:S(2)}, u32[]{:S(2)}) %collective-permute-start.12) | collective-permute-done | bytes 524320 | tf_op jit(solution)/shard_map/ppermute | solution.py:48
  64.2 0.0 collective-permute-done.7.g1
  64.2 2.4 %collective-permute-done.13.y3 = bf16[8,128,256]{2,1,0:T(8,128)(2,1)S(1)} collective-permute-done((bf16[8,128,256]{2,1,0:T(8,128)(2,1)S(1)}, bf16[8,128,256]{2,1,0:T(8,128)(2,1)S(1)}, u32[]{:S(2)}, u32[]{:S(2)}) %collective-permute-start.13) | collective-permute-done | bytes 524320 | tf_op jit(solution)/shard_map/ppermute | solution.py:48
  66.6 0.0 collective-permute-done.9.g3
  66.6 5.8 %shard_map.37 = f32[512,128]{1,0:T(8,128)S(1)} custom-call(bf16[256,1536]{1,0:T(8,128)(2,1)S(1)} %collective-permute-done.2.h0, bf16[256,1536]{1,0:T(8,128)(2,1)S(1)} %collective-permute-done.3.h1, bf16[256,1536]{1,0:T(8,128)(2,1)S(1)} %collective-permute-done.4.h2, bf16[256,1536]{1,0:T(8,128)(2,1)} %collective-permute-done.5.h3, ...), custom_call_target="tpu_custom_call" | custom-call | flops 3400000000 | bytes 9000000 | tf_op jit(solution)/shard_map/pallas_call | solution.py:83
  72.4 20.4 %all_to_all.10 = f32[32,16,128]{2,1,0:T(8,128)S(1)} all-to-all(f32[32,16,128]{2,1,0:T(8,128)S(1)} %bitcast.4), channel_id=1, replica_groups=mesh['yh'=2,'x'=4,'yl'=2,'z'=8,'c'=2] {'yh','yl','z'}, dimensions={0} | all-to-all | bytes 524288 | tf_op jit(solution)/shard_map/all_to_all | solution.py:114
  92.8 0.6 reduce_sum.9
  (8 shorter events, 0.0 us)
Async XLA Ops:
  0.0 7.9 %copy-start.1 = (bf16[2,256,128]{2,1,0:T(8,128)(2,1)S(1)}, bf16[2,256,128]{2,1,0:T(8,128)(2,1)}, u32[]{:S(2)}) copy-start(bf16[2,256,128]{2,1,0:T(8,128)(2,1)} %constant.14.clone) | copy-start | bytes 393220
  0.0 8.1 %collective-permute-start.2 = (bf16[256,1536]{1,0:T(8,128)(2,1)}, bf16[256,1536]{1,0:T(8,128)(2,1)S(1)}, u32[]{:S(2)}, u32[]{:S(2)}) collective-permute-start(bf16[256,1536]{1,0:T(8,128)(2,1)} %param.3), channel_id=1, source_target_pairs={{0,0},{1,128},{2,2},{3,130},{4,4},{5,132},{6,6},{7,134},{8,8},{9,1... | collective-permute-start | bytes 2359304 | tf_op jit(solution)/shard_map/ppermute | solution.py:48
  2.8 0.7 collective-permute-start
  3.4 4.4 %collective-permute-start.1 = (bf16[256,128]{1,0:T(8,128)(2,1)S(1)}, bf16[256,128]{1,0:T(8,128)(2,1)S(1)}, u32[]{:S(2)}, u32[]{:S(2)}) collective-permute-start(bf16[256,128]{1,0:T(8,128)(2,1)S(1)} %collective-permute-done), channel_id=1, source_target_pairs={{0,1},{1,0},{2,3},{3,2},{4,5},{5,4},{6,7},{7,6},{8,9},{9,8},{10,11... | collective-permute-start | bytes 196616 | tf_op jit(solution)/shard_map/ppermute | solution.py:48
  8.1 23.4 %collective-permute-start.3 = (bf16[256,1536]{1,0:T(8,128)(2,1)S(1)}, bf16[256,1536]{1,0:T(8,128)(2,1)S(1)}, u32[]{:S(2)}, u32[]{:S(2)}) collective-permute-start(bf16[256,1536]{1,0:T(8,128)(2,1)S(1)} %collective-permute-done.2.h0), channel_id=1, source_target_pairs={{0,32},{1,97},{2,34},{3,99},{4,36},{5,101},{6,38},{7,103},{8,40},{... | collective-permute-start | bytes 2359304 | tf_op jit(solution)/shard_map/ppermute | solution.py:48
  16.5 15.5 %copy-start = (bf16[1536,128]{1,0:T(8,128)(2,1)S(1)}, bf16[1536,128]{1,0:T(8,128)(2,1)}, u32[]{:S(2)}) copy-start(bf16[1536,128]{1,0:T(8,128)(2,1)} %pair.1) | copy-start | bytes 1179652
  16.5 28.3 %all-to-all-start = ((bf16[8,128,256]{2,1,0:T(8,128)(2,1)}), bf16[8,128,256]{2,1,0:T(8,128)(2,1)S(1)}, u32[]{:S(2)}, u32[]{:S(2)}) async-start(bf16[8,128,256]{2,1,0:T(8,128)(2,1)} %broadcast_in_dim.2), calls=%async_computation | async-start | bytes 1048576 | tf_op jit(solution)/shard_map/all_to_all | solution.py:107
  28.9 20.4 %collective-permute-start.4 = (bf16[256,1536]{1,0:T(8,128)(2,1)S(1)}, bf16[256,1536]{1,0:T(8,128)(2,1)S(1)}, u32[]{:S(2)}, u32[]{:S(2)}) collective-permute-start(bf16[256,1536]{1,0:T(8,128)(2,1)S(1)} %collective-permute-done.2.h0), channel_id=1, source_target_pairs={{0,96},{1,33},{2,98},{3,35},{4,100},{5,37},{6,102},{7,39},{8,104},... | collective-permute-start | bytes 2359304 | tf_op jit(solution)/shard_map/ppermute | solution.py:48
  31.5 18.3 %collective-permute-start.5 = (bf16[256,1536]{1,0:T(8,128)(2,1)S(1)}, bf16[256,1536]{1,0:T(8,128)(2,1)}, u32[]{:S(2)}, u32[]{:S(2)}) collective-permute-start(bf16[256,1536]{1,0:T(8,128)(2,1)S(1)} %collective-permute-done.3.h1), channel_id=1, source_target_pairs={{0,32},{1,97},{2,34},{3,99},{4,36},{5,101},{6,38},{7,103},{8,40},{... | collective-permute-start | bytes 2359304 | tf_op jit(solution)/shard_map/ppermute | solution.py:48
  31.8 18.1 %collective-permute-start.6 = (bf16[256,1536]{1,0:T(8,128)(2,1)S(1)}, bf16[256,1536]{1,0:T(8,128)(2,1)}, u32[]{:S(2)}, u32[]{:S(2)}) collective-permute-start(bf16[256,1536]{1,0:T(8,128)(2,1)S(1)} %collective-permute-done.2.h0), channel_id=1, source_target_pairs={{0,1},{1,0},{2,3},{3,2},{4,5},{5,4},{6,7},{7,6},{8,9},{9,8},{10,11... | collective-permute-start | bytes 2359304 | tf_op jit(solution)/shard_map/ppermute | solution.py:48
  32.0 17.2 %collective-permute-start.10 = (bf16[1536,128]{1,0:T(8,128)(2,1)S(1)}, bf16[1536,128]{1,0:T(8,128)(2,1)}, u32[]{:S(2)}, u32[]{:S(2)}) collective-permute-start(bf16[1536,128]{1,0:T(8,128)(2,1)S(1)} %copy-done), channel_id=1, source_target_pairs={{0,1},{1,0},{2,3},{3,2},{4,5},{5,4},{6,7},{7,6},{8,9},{9,8},{10,11... | collective-permute-start | bytes 1179656 | tf_op jit(solution)/shard_map/ppermute | solution.py:48
  44.8 11.4 %collective-permute-start.11 = (bf16[8,128,256]{2,1,0:T(8,128)(2,1)S(1)}, bf16[8,128,256]{2,1,0:T(8,128)(2,1)S(1)}, u32[]{:S(2)}, u32[]{:S(2)}) collective-permute-start(bf16[8,128,256]{2,1,0:T(8,128)(2,1)S(1)} %all-to-all-done.y0), channel_id=1, source_target_pairs={{0,16},{1,145},{2,18},{3,147},{4,20},{5,149},{6,22},{7,151},{8,24}... | collective-permute-start | bytes 1572872 | tf_op jit(solution)/shard_map/ppermute | solution.py:48
  49.3 15.0 %collective-permute-start.8 = (bf16[256,1536]{1,0:T(8,128)(2,1)S(1)}, bf16[256,1536]{1,0:T(8,128)(2,1)S(1)}, u32[]{:S(2)}, u32[]{:S(2)}) collective-permute-start(bf16[256,1536]{1,0:T(8,128)(2,1)S(1)} %collective-permute-done.4.h2), channel_id=1, source_target_pairs={{0,1},{1,0},{2,3},{3,2},{4,5},{5,4},{6,7},{7,6},{8,9},{9,8},{10,11... | collective-permute-start | bytes 2359304 | tf_op jit(solution)/shard_map/ppermute | solution.py:48
  49.3 14.9 %collective-permute-start.7 = (bf16[256,1536]{1,0:T(8,128)(2,1)S(1)}, bf16[256,1536]{1,0:T(8,128)(2,1)S(1)}, u32[]{:S(2)}, u32[]{:S(2)}) collective-permute-start(bf16[256,1536]{1,0:T(8,128)(2,1)S(1)} %collective-permute-done.3.h1), channel_id=1, source_target_pairs={{0,1},{1,0},{2,3},{3,2},{4,5},{5,4},{6,7},{7,6},{8,9},{9,8},{10,11... | collective-permute-start | bytes 2359304 | tf_op jit(solution)/shard_map/ppermute | solution.py:48
  49.8 16.8 %collective-permute-start.9 = (bf16[256,1536]{1,0:T(8,128)(2,1)}, bf16[256,1536]{1,0:T(8,128)(2,1)S(1)}, u32[]{:S(2)}, u32[]{:S(2)}) collective-permute-start(bf16[256,1536]{1,0:T(8,128)(2,1)} %collective-permute-done.5.h3), channel_id=1, source_target_pairs={{0,1},{1,0},{2,3},{3,2},{4,5},{5,4},{6,7},{7,6},{8,9},{9,8},{10,11... | collective-permute-start | bytes 2359304 | tf_op jit(solution)/shard_map/ppermute | solution.py:48
  49.9 14.3 %collective-permute-start.12 = (bf16[8,128,256]{2,1,0:T(8,128)(2,1)S(1)}, bf16[8,128,256]{2,1,0:T(8,128)(2,1)S(1)}, u32[]{:S(2)}, u32[]{:S(2)}) collective-permute-start(bf16[8,128,256]{2,1,0:T(8,128)(2,1)S(1)} %all-to-all-done.y0), channel_id=1, source_target_pairs={{0,144},{1,17},{2,146},{3,19},{4,148},{5,21},{6,150},{7,23},{8,152... | collective-permute-start | bytes 1572872 | tf_op jit(solution)/shard_map/ppermute | solution.py:48
  56.3 10.4 %collective-permute-start.13 = (bf16[8,128,256]{2,1,0:T(8,128)(2,1)S(1)}, bf16[8,128,256]{2,1,0:T(8,128)(2,1)S(1)}, u32[]{:S(2)}, u32[]{:S(2)}) collective-permute-start(bf16[8,128,256]{2,1,0:T(8,128)(2,1)S(1)} %collective-permute-done.11.y1), channel_id=1, source_target_pairs={{0,16},{1,145},{2,18},{3,147},{4,20},{5,149},{6,22},{7,151},{8,24}... | collective-permute-start | bytes 1572872 | tf_op jit(solution)/shard_map/ppermute | solution.py:48

commit v3 on v2

v3 whole, which is shorter than its diff:
```python
import jax
import jax.numpy as jnp
import numpy as np
from jax import lax
from jax.experimental import pallas as pl
from jax.experimental.pallas import tpu as pltpu
from jax.sharding import Mesh, PartitionSpec as P

PAN_DEV = 128
AXES = ("yh", "x", "yl", "z", "c")
SIZES = (2, 4, 2, 8, 2)
TILE = 512


def perm_of(move, only=lambda yh, c: True):
    pairs = []
    for s in range(256):
        yh, x, yl, z, c = (int(i) for i in np.unravel_index(s, SIZES))
        if only(yh, c):
            x, y, z, c = move(x, 2 * yh + yl, z, c)
            y = y % 4
            pairs.append((s, int(np.ravel_multi_index((y // 2, x % 4, y % 2, z % 8, c), SIZES))))
    return pairs


def is_own(y, c):
    return c == y // 2


def own(yh, c):
    return c == yh


CORE = perm_of(lambda x, y, z, c: (x, y, z, 1 - c))
SPREAD, SPREAD_FAR = (perm_of(lambda x, y, z, c: (z // 2, y, 2 * x + z % 2 + d, c)) for d in (0, 4))
TRADE = perm_of(lambda x, y, z, c: (x, y, z, c) if is_own(y, c) else (x, y + 2, z, 1 - c))


def x_step(d):
    return perm_of(lambda x, y, z, c: (x + d if c == 0 else x - d, y, z, c))


def z_step(d):
    return perm_of(lambda x, y, z, c: (x, y, z + d if c == 0 else z - d, c))


def y_step(d):
    return perm_of(lambda x, y, z, c: (x, y + d if c == 0 else y - d, z, c))


def send(a, perm):
    return lax.ppermute(a, AXES, perm)


def picker():
    m = np.zeros((2, 4, 2, 16, 2, 4, 16), np.float32)
    for c in range(2):
        for r in range(2):
            for j in range(4):
                for i in range(16):
                    m[c, j, c ^ r, i, r, j, i] = 1
    return m.reshape(2, 128, 128)


def place(blocks, ref, first=0):
    z, c = lax.axis_index("z"), lax.axis_index("c")
    side = 2 * c - 1
    for i in range(ref.shape[0]):
        off = (0, side, -side, 2 * side)[(first + i) // 2] + 4 * (i % 2)
        blocks[lax.rem(z + off + 8, 8)] = ref[i]


def first_kernel(h0, h1, h2, g0, g1, g2, *rest):
    *panel, out, blocks = rest
    yh, x, yl, c = (lax.axis_index(a) for a in ("yh", "x", "yl", "c"))
    side = 2 * c - 1
    for dy, ref in zip((0, side, -side), panel):
        place(blocks.at[lax.rem(2 * yh + yl + dy + 4, 4)], ref)

    def product(whole, partial, sign):
        @pl.loop(0, out.shape[1] // TILE)
        def _(t):
            at = pl.ds(pl.multiple_of(t * TILE, TILE), TILE)
            gram, more = 0, 0
            for dx, cols, others in zip((0, sign * side, -sign * side), whole, partial):
                z2 = 2 * lax.rem(x + dx + 4, 4)
                rows = blocks[pl.ds(2 * yh, 2), pl.ds(z2, 2)].reshape(512, 256)
                gram += jnp.dot(rows, cols[:, at], preferred_element_type=jnp.float32)
                z2 = 2 * lax.rem(x - dx + 4, 4)
                rows = blocks[2 * (1 - yh) + 1 - yl, pl.ds(z2, 2)].reshape(256, 256)
                more += jnp.dot(rows, others[:, at], preferred_element_type=jnp.float32)
            out[:, at] = gram
            out[pl.ds(pl.multiple_of((1 - yl) * 256, 256), 256), at] += more

    @pl.when(c == yh)
    def _():
        product((h0, h1, h2), (g0, g1, g2), 1)

    @pl.when(c != yh)
    def _():
        product((g0, g1, g2), (h0, h1, h2), -1)


def last_kernel(gram, blocks, h0, h1, h2, h3, g0, g1, g2, g3, pair, cspair, y3, y4, out, last):
    yh, x, yl, c = (lax.axis_index(a) for a in ("yh", "x", "yl", "c"))
    side = 2 * c - 1
    place(last, y3)
    place(last, y4, 4)
    out[...] = jnp.zeros_like(out)
    z2 = 2 * lax.rem(x + 2, 4)

    def product(whole, partial, weights, sign):
        @pl.loop(0, gram.shape[1] // TILE)
        def _(t):
            at = pl.ds(pl.multiple_of(t * TILE, TILE), TILE)
            here, there = (pl.ds(pl.multiple_of(r * 256, 256), 256) for r in (yl, 1 - yl))

            def add(values, rows, cols):
                return values + jnp.dot(rows.reshape(256, 256), cols[:, at], preferred_element_type=jnp.float32)

            def contract(rows, values):
                squared = (values * values).astype(jnp.bfloat16)
                out[rows, :] += jnp.dot(squared, weights[at, :], preferred_element_type=jnp.float32)

            values = add(gram[there, at], blocks[2 * yh + 1 - yl, pl.ds(z2, 2)], whole)
            contract(there, add(values, blocks[2 * (1 - yh) + 1 - yl, pl.ds(z2, 2)], partial[3]))
            values = add(gram[here, at], blocks[2 * yh + yl, pl.ds(z2, 2)], whole)
            for dx, cols in zip((0, sign * side, -sign * side, 2), partial):
                values = add(values, last[pl.ds(2 * lax.rem(x + dx + 4, 4), 2)], cols)
            contract(here, values)

    @pl.when(c == yh)
    def _():
        product(h3, (g0, g1, g2, g3), pair, -1)

    @pl.when(c != yh)
    def _():
        product(g3, (h0, h1, h2, h3), cspair, 1)


def call(kernel, shapes, scratch, flops, *operands):
    return pl.pallas_call(
        kernel,
        out_shape=[jax.ShapeDtypeStruct(*shape) for shape in shapes],
        in_specs=[pl.BlockSpec(memory_space=pltpu.VMEM)] * len(operands),
        out_specs=[pl.BlockSpec(memory_space=pltpu.VMEM)] * len(shapes),
        scratch_shapes=scratch,
        compiler_params=pltpu.CompilerParams(vmem_limit_bytes=24 * 2**20),
        cost_estimate=pl.CostEstimate(flops=flops, bytes_accessed=9_000_000, transcendentals=0),
    )(*operands)


def on_device(collocation, pair_tensor):
    c = lax.axis_index("c")

    pick = lax.dynamic_index_in_dim(jnp.asarray(picker(), jnp.bfloat16), c, keepdims=False)
    picked = lax.dot_general(
        pick, collocation[:, :PAN_DEV], (((0,), (1,)), ((), ())), preferred_element_type=jnp.float32
    ).astype(jnp.bfloat16)
    got = [send(picked, SPREAD), send(picked, SPREAD_FAR)]
    h0 = send(collocation, TRADE)
    cspair = send(pair_tensor, CORE)
    *got, h0 = lax.optimization_barrier((*got, h0))
    parts = [(a[:64], send(a, CORE)[64:]) for a in got]
    block = jnp.stack([jnp.where(c == 0, jnp.concatenate([a, b]), jnp.concatenate([b, a])) for a, b in parts])
    ring = jnp.concatenate([block, send(block, z_step(1)), send(block, z_step(-1)), send(block, z_step(2))])

    h1, h2 = send(h0, x_step(1)), send(h0, x_step(-1))
    y1, y2 = send(ring, y_step(1)), send(ring, y_step(-1))
    h1, h2, y1, y2, cspair = lax.optimization_barrier((h1, h2, y1, y2, cspair))
    h3 = send(h1, x_step(1))
    y3, y4 = send(y1[:4], y_step(1)), send(y2[4:], y_step(-1))
    h = [h0, h1, h2]
    g = [send(a, CORE) for a in h]
    shapes = ((512, 1536), jnp.float32), ((4, 8, 128, 256), jnp.bfloat16)
    gram, blocks = call(first_kernel, shapes, [], 1_800_000_000, *h, *g, ring, y1, y2)
    h3, y3, y4, gram = lax.optimization_barrier((h3, y3, y4, gram))
    h.append(h3)
    g.append(send(h3, CORE))
    shapes = (((512, 128), jnp.float32),)
    scratch = [pltpu.VMEM((8, 128, 256), jnp.bfloat16)]
    (part,) = call(last_kernel, shapes, scratch, 1_600_000_000, gram, blocks, *h, *g, pair_tensor, cspair, y3, y4)
    parts = lax.all_to_all(part.reshape(32, 16, 128), ("yh", "yl", "z"), 0, 0)
    return parts.sum(0)


def solution(mesh):
    return jax.shard_map(
        on_device,
        mesh=Mesh(mesh.devices.reshape(SIZES), AXES),
        in_specs=(P(("yh", "x"), ("yl", "z", "c")), P(("yl", "z", "c"), None)),
        out_specs=P(AXES, None),
        check_vma=False,
    )
```

time: 94.7 us -> 88.3 us (0.932); the launches traced: 93.4 us -> 88 us
  waiting for transfers between devices: 32.1 us -> 29.3 us
  blocking collectives: 20.4 us -> 18.7 us
  local copies, waits for them, and re-layouts: 1.7 us -> 0.08 us
    all_to_all x1 -> x0, waiting for transfers between devices: 12.5 us -> none  [on_device(): lax.all_to_all(jnp.broadcast_to(block[None], (8, 128, 256)), 'z', 0, 0)]
    ppermute x14 -> x20, starting transfers between devices: 20.3 us -> 32.7 us  [send(): return lax.ppermute(a, AXES, perm)]
    all_to_all x1 -> x0, starting transfers between devices: 12.3 us -> none  [on_device(): lax.all_to_all(jnp.broadcast_to(block[None], (8, 128, 256)), 'z', 0, 0)]
    ppermute x14 -> x20, waiting for transfers between devices: 19.6 us -> 29.3 us  [send(): return lax.ppermute(a, AXES, perm)]
    all_to_all x1, blocking collectives: 20.4 us -> 18.7 us  [on_device(): parts = lax.all_to_all(part.reshape(32, 16, 128), ('yh', 'yl', 'z'), 0, 0)]
    pallas_call x1 -> x2, Pallas kernels: 5.79 us -> 5.35 us  [call(): pl.pallas_call(kernel, out_shape=[jax.ShapeDtypeStruct(*shape) for shape...]
  transfers between devices with their start and end apart: 15 -> 20, of which waited for: 6 -> 9; matrix products, arithmetic and copies ran while one was open for 2% -> 1% of each run, Pallas kernels for 0% -> 3%
where the time goes in v3:
time: 88.3 us; the launch traced here: 88 us
  starting transfers between devices  32.7 us (37%)
  waiting for transfers between devices  29.3 us (33%)
  blocking collectives  18.7 us (21%)
  Pallas kernels  5.35 us (6%)
  matrix products  1.05 us (1%)
    ppermute x20, starting transfers between devices, send(): return lax.ppermute(a, AXES, perm)  32.7 us
    ppermute x20, waiting for transfers between devices, send(): return lax.ppermute(a, AXES, perm)  29.3 us
    all_to_all x1, blocking collectives, on_device(): parts = lax.all_to_all(part.reshape(32, 16, 128), ('yh', 'yl', 'z'), 0, 0)  18.7 us
    pallas_call x2, Pallas kernels, call(): pl.pallas_call(kernel, out_shape=[jax.ShapeDtypeStruct(*shape) for shape...  5.35 us
  transfers between devices with their start and end apart: 20, of which 9 were waited for; matrix products, arithmetic and copies ran while one was open for 1% of the time, Pallas kernels for 3%

profile of v3, /device:TPU:32, one launch (start us, length us, event | category | flops | bytes accessed | tf_op | source)
XLA Modules:
  0.0 88.0 jit_solution(10602350831595101971)
XLA Ops:
  0.0 1.8 %collective-permute-start.2 = (bf16[256,1536]{1,0:T(8,128)(2,1)}, bf16[256,1536]{1,0:T(8,128)(2,1)S(1)}, u32[]{:S(2)}, u32[]{:S(2)}) collective-permute-start(bf16[256,1536]{1,0:T(8,128)(2,1)} %param.3), channel_id=1, source_target_pairs={{0,0},{1,128},{2,2},{3,130},{4,4},{5,132},{6,6},{7,134},{8,8},{9,1... | collective-permute-start | bytes 2359304 | tf_op jit(solution)/shard_map/ppermute | solution.py:52
  1.8 1.0 %convolution_convert_fusion = bf16[128,256]{1,0:T(8,128)(2,1)S(1)} fusion(bf16[256,1536]{1,0:T(8,128)(2,1)} %param.3, bf16[2,128,128]{2,1,0:T(8,128)(2,1)} %constant.15.clone, s32[]{:T(128)S(6)} %select_n.30), kind=kOutput, calls=%fused_computation | convolution fusion | flops 8421376 | bytes 163844 | tf_op jit(solution)/shard_map/dot_general | solution.py:157
  2.8 0.7 collective-permute-start
  3.5 9.7 %collective-permute-start.1 = (bf16[128,256]{1,0:T(8,128)(2,1)S(1)}, bf16[128,256]{1,0:T(8,128)(2,1)S(1)}, u32[]{:S(2)}, u32[]{:S(2)}) collective-permute-start(bf16[128,256]{1,0:T(8,128)(2,1)S(1)} %convolution_convert_fusion), channel_id=1, source_target_pairs={{0,8},{1,9},{2,10},{3,11},{4,40},{5,41},{6,42},{7,43},{8,72},{9,73... | collective-permute-start | bytes 196616 | tf_op jit(solution)/shard_map/ppermute | solution.py:52
  13.2 3.1 %collective-permute-done.1 = bf16[128,256]{1,0:T(8,128)(2,1)S(1)} collective-permute-done((bf16[128,256]{1,0:T(8,128)(2,1)S(1)}, bf16[128,256]{1,0:T(8,128)(2,1)S(1)}, u32[]{:S(2)}, u32[]{:S(2)}) %collective-permute-start.1) | collective-permute-done | bytes 65568 | tf_op jit(solution)/shard_map/ppermute | solution.py:52
  16.3 2.3 %collective-permute-start.5 = (bf16[128,256]{1,0:T(8,128)(2,1)S(1)}, bf16[128,256]{1,0:T(8,128)(2,1)S(1)}, u32[]{:S(2)}, u32[]{:S(2)}) collective-permute-start(bf16[128,256]{1,0:T(8,128)(2,1)S(1)} %collective-permute-done), channel_id=1, source_target_pairs={{0,1},{1,0},{2,3},{3,2},{4,5},{5,4},{6,7},{7,6},{8,9},{9,8},{10,11... | collective-permute-start | bytes 196616 | tf_op jit(solution)/shard_map/ppermute | solution.py:52
  18.7 0.1 collective-permute-start.6
  18.8 0.8 collective-permute-done.5
  19.6 0.3 collective-permute-done.6
  20.0 0.9 %collective-permute-start.7 = (bf16[2,128,256]{2,1,0:T(8,128)(2,1)S(1)}, bf16[2,128,256]{2,1,0:T(8,128)(2,1)S(1)}, u32[]{:S(2)}, u32[]{:S(2)}) collective-permute-start(bf16[2,128,256]{2,1,0:T(8,128)(2,1)S(1)} %pad_maximum_fusion), channel_id=1, source_target_pairs={{0,2},{1,15},{2,4},{3,1},{4,6},{5,3},{6,8},{7,5},{8,10},{9,7},{10,... | collective-permute-start | bytes 393224 | tf_op jit(solution)/shard_map/ppermute | solution.py:52
  20.9 1.2 %collective-permute-start.8 = (bf16[2,128,256]{2,1,0:T(8,128)(2,1)S(1)}, bf16[2,128,256]{2,1,0:T(8,128)(2,1)S(1)}, u32[]{:S(2)}, u32[]{:S(2)}) collective-permute-start(bf16[2,128,256]{2,1,0:T(8,128)(2,1)S(1)} %pad_maximum_fusion), channel_id=1, source_target_pairs={{0,14},{1,3},{2,0},{3,5},{4,2},{5,7},{6,4},{7,9},{8,6},{9,11},{10,... | collective-permute-start | bytes 393224 | tf_op jit(solution)/shard_map/ppermute | solution.py:52
  22.1 0.6 collective-permute-start.3
  22.7 4.7 %collective-permute-start.4 = (bf16[256,1536]{1,0:T(8,128)(2,1)S(1)}, bf16[256,1536]{1,0:T(8,128)(2,1)S(1)}, u32[]{:S(2)}, u32[]{:S(2)}) collective-permute-start(bf16[256,1536]{1,0:T(8,128)(2,1)S(1)} %collective-permute-done.2.h0), channel_id=1, source_target_pairs={{0,96},{1,33},{2,98},{3,35},{4,100},{5,37},{6,102},{7,39},{8,104},... | collective-permute-start | bytes 2359304 | tf_op jit(solution)/shard_map/ppermute | solution.py:52
  27.3 2.5 %collective-permute-start.9 = (bf16[2,128,256]{2,1,0:T(8,128)(2,1)S(1)}, bf16[2,128,256]{2,1,0:T(8,128)(2,1)S(1)}, u32[]{:S(2)}, u32[]{:S(2)}) collective-permute-start(bf16[2,128,256]{2,1,0:T(8,128)(2,1)S(1)} %pad_maximum_fusion), channel_id=1, source_target_pairs={{0,4},{1,13},{2,6},{3,15},{4,8},{5,1},{6,10},{7,3},{8,12},{9,5},{1... | collective-permute-start | bytes 393224 | tf_op jit(solution)/shard_map/ppermute | solution.py:52
  29.9 6.0 %collective-permute-done.9 = bf16[2,128,256]{2,1,0:T(8,128)(2,1)S(1)} collective-permute-done((bf16[2,128,256]{2,1,0:T(8,128)(2,1)S(1)}, bf16[2,128,256]{2,1,0:T(8,128)(2,1)S(1)}, u32[]{:S(2)}, u32[]{:S(2)}) %collective-permute-start.9) | collective-permute-done | bytes 131104 | tf_op jit(solution)/shard_map/ppermute | solution.py:52
  35.8 0.8 collective-permute-start.10
  36.6 2.6 %collective-permute-start.11 = (bf16[8,128,256]{2,1,0:T(8,128)(2,1)S(1)}, bf16[8,128,256]{2,1,0:T(8,128)(2,1)S(1)}, u32[]{:S(2)}, u32[]{:S(2)}) collective-permute-start(bf16[8,128,256]{2,1,0:T(8,128)(2,1)S(1)} %constant_dynamic-update-slice_fusion.rest_0_), channel_id=1, source_target_pairs={{0,144},{1,17},{2,146},{3,19},{4,148},{5,21},{6,150},{7,23},{8,152... | collective-permute-start | bytes 1572872 | tf_op jit(solution)/shard_map/ppermute | solution.py:52
  39.2 1.9 %collective-permute-done.12.cspair = bf16[1536,128]{1,0:T(8,128)(2,1)S(1)} collective-permute-done((bf16[1536,128]{1,0:T(8,128)(2,1)}, bf16[1536,128]{1,0:T(8,128)(2,1)S(1)}, u32[]{:S(2)}, u32[]{:S(2)}) %collective-permute-start.12) | collective-permute-done | bytes 393248 | tf_op jit(solution)/shard_map/ppermute | solution.py:52
  41.1 0.1 collective-permute-start.16
  41.2 8.5 %collective-permute-done.10.rest_1_ = bf16[8,128,256]{2,1,0:T(8,128)(2,1)S(1)} collective-permute-done((bf16[8,128,256]{2,1,0:T(8,128)(2,1)S(1)}, bf16[8,128,256]{2,1,0:T(8,128)(2,1)S(1)}, u32[]{:S(2)}, u32[]{:S(2)}) %collective-permute-start.10) | collective-permute-done | bytes 524320 | tf_op jit(solution)/shard_map/ppermute | solution.py:52
  49.7 0.1 collective-permute-start.17
  49.8 0.5 collective-permute-start.18
  50.3 0.7 collective-permute-start.13
  51.1 0.1 collective-permute-start.14
  51.2 3.5 %collective-permute-start.15 = (bf16[4,128,256]{2,1,0:T(8,128)(2,1)S(1)}, bf16[4,128,256]{2,1,0:T(8,128)(2,1)S(1)}, u32[]{:S(2)}, u32[]{:S(2)}) collective-permute-start(bf16[4,128,256]{2,1,0:T(8,128)(2,1)S(1)} %slice.27), channel_id=1, source_target_pairs={{0,144},{1,17},{2,146},{3,19},{4,148},{5,21},{6,150},{7,23},{8,152... | collective-permute-start | bytes 786440 | tf_op jit(solution)/shard_map/ppermute | solution.py:52
  54.7 2.5 %shard_map.37 = (f32[512,1536]{1,0:T(8,128)S(1)}, bf16[4,8,128,256]{3,2,1,0:T(8,128)(2,1)S(1)}) custom-call(bf16[256,1536]{1,0:T(8,128)(2,1)S(1)} %collective-permute-done.2.h0, bf16[256,1536]{1,0:T(8,128)(2,1)S(1)} %collective-permute-done.3.h1, bf16[256,1536]{1,0:T(8,128)(2,1)S(1)} %collective-permute-done.4.h2, ...), custom_call_target="tpu_custom_call" | custom-call | flops 1800000000 | bytes 9000000 | tf_op jit(solution)/shard_map/pallas_call | solution.py:142
  57.2 2.9 %collective-permute-done.14.y3 = bf16[4,128,256]{2,1,0:T(8,128)(2,1)S(1)} collective-permute-done((bf16[4,128,256]{2,1,0:T(8,128)(2,1)S(1)}, bf16[4,128,256]{2,1,0:T(8,128)(2,1)S(1)}, u32[]{:S(2)}, u32[]{:S(2)}) %collective-permute-start.14) | collective-permute-done | bytes 262176 | tf_op jit(solution)/shard_map/ppermute | solution.py:52
  60.0 3.5 %collective-permute-done.13.h3 = bf16[256,1536]{1,0:T(8,128)(2,1)S(1)} collective-permute-done((bf16[256,1536]{1,0:T(8,128)(2,1)S(1)}, bf16[256,1536]{1,0:T(8,128)(2,1)S(1)}, u32[]{:S(2)}, u32[]{:S(2)}) %collective-permute-start.13) | collective-permute-done | bytes 786464 | tf_op jit(solution)/shard_map/ppermute | solution.py:52
  63.5 2.3 %collective-permute-done.19.g3 = bf16[256,1536]{1,0:T(8,128)(2,1)S(1)} collective-permute-done((bf16[256,1536]{1,0:T(8,128)(2,1)S(1)}, bf16[256,1536]{1,0:T(8,128)(2,1)S(1)}, u32[]{:S(2)}, u32[]{:S(2)}) %collective-permute-start.19) | collective-permute-done | bytes 786464 | tf_op jit(solution)/shard_map/ppermute | solution.py:52
  65.8 2.9 %shard_map.38 = f32[512,128]{1,0:T(8,128)S(1)} custom-call(f32[512,1536]{1,0:T(8,128)S(1)} %get-tuple-element.27.gram, bf16[4,8,128,256]{3,2,1,0:T(8,128)(2,1)S(1)} %get-tuple-element.28.blocks, bf16[256,1536]{1,0:T(8,128)(2,1)S(1)} %collective-permute-done.2.h0, bf16[256,1536]{1,0:T(8,128)(2,1)S(1)} %collective-permute-done.3.h1, ...), custom_call_target="tpu_custom_call" | custom-call | flops 1600000000 | bytes 9000000 | tf_op jit(solution)/shard_map/pallas_call | solution.py:142
  68.7 18.7 %all_to_all.5 = f32[32,16,128]{2,1,0:T(8,128)S(1)} all-to-all(f32[32,16,128]{2,1,0:T(8,128)S(1)} %bitcast.12), channel_id=1, replica_groups=mesh['yh'=2,'x'=4,'yl'=2,'z'=8,'c'=2] {'yh','yl','z'}, dimensions={0} | all-to-all | bytes 524288 | tf_op jit(solution)/shard_map/all_to_all | solution.py:183
  87.4 0.6 reduce_sum.9
  (26 shorter events, 0.2 us)
Async XLA Ops:
  0.0 16.3 %collective-permute-start.2 = (bf16[256,1536]{1,0:T(8,128)(2,1)}, bf16[256,1536]{1,0:T(8,128)(2,1)S(1)}, u32[]{:S(2)}, u32[]{:S(2)}) collective-permute-start(bf16[256,1536]{1,0:T(8,128)(2,1)} %param.3), channel_id=1, source_target_pairs={{0,0},{1,128},{2,2},{3,130},{4,4},{5,132},{6,6},{7,134},{8,8},{9,1... | collective-permute-start | bytes 2359304 | tf_op jit(solution)/shard_map/ppermute | solution.py:52
  2.8 10.4 %collective-permute-start = (bf16[128,256]{1,0:T(8,128)(2,1)S(1)}, bf16[128,256]{1,0:T(8,128)(2,1)S(1)}, u32[]{:S(2)}, u32[]{:S(2)}) collective-permute-start(bf16[128,256]{1,0:T(8,128)(2,1)S(1)} %convolution_convert_fusion), channel_id=1, source_target_pairs={{0,0},{1,1},{2,2},{3,3},{4,32},{5,33},{6,34},{7,35},{8,64},{9,65},... | collective-permute-start | bytes 196616 | tf_op jit(solution)/shard_map/ppermute | solution.py:52
  3.5 12.8 %collective-permute-start.1 = (bf16[128,256]{1,0:T(8,128)(2,1)S(1)}, bf16[128,256]{1,0:T(8,128)(2,1)S(1)}, u32[]{:S(2)}, u32[]{:S(2)}) collective-permute-start(bf16[128,256]{1,0:T(8,128)(2,1)S(1)} %convolution_convert_fusion), channel_id=1, source_target_pairs={{0,8},{1,9},{2,10},{3,11},{4,40},{5,41},{6,42},{7,43},{8,72},{9,73... | collective-permute-start | bytes 196616 | tf_op jit(solution)/shard_map/ppermute | solution.py:52
  16.3 3.2 %collective-permute-start.5 = (bf16[128,256]{1,0:T(8,128)(2,1)S(1)}, bf16[128,256]{1,0:T(8,128)(2,1)S(1)}, u32[]{:S(2)}, u32[]{:S(2)}) collective-permute-start(bf16[128,256]{1,0:T(8,128)(2,1)S(1)} %collective-permute-done), channel_id=1, source_target_pairs={{0,1},{1,0},{2,3},{3,2},{4,5},{5,4},{6,7},{7,6},{8,9},{9,8},{10,11... | collective-permute-start | bytes 196616 | tf_op jit(solution)/shard_map/ppermute | solution.py:52
  18.7 1.3 %collective-permute-start.6 = (bf16[128,256]{1,0:T(8,128)(2,1)S(1)}, bf16[128,256]{1,0:T(8,128)(2,1)S(1)}, u32[]{:S(2)}, u32[]{:S(2)}) collective-permute-start(bf16[128,256]{1,0:T(8,128)(2,1)S(1)} %collective-permute-done.1), channel_id=1, source_target_pairs={{0,1},{1,0},{2,3},{3,2},{4,5},{5,4},{6,7},{7,6},{8,9},{9,8},{10,11... | collective-permute-start | bytes 196616 | tf_op jit(solution)/shard_map/ppermute | solution.py:52
  20.0 9.9 %collective-permute-start.7 = (bf16[2,128,256]{2,1,0:T(8,128)(2,1)S(1)}, bf16[2,128,256]{2,1,0:T(8,128)(2,1)S(1)}, u32[]{:S(2)}, u32[]{:S(2)}) collective-permute-start(bf16[2,128,256]{2,1,0:T(8,128)(2,1)S(1)} %pad_maximum_fusion), channel_id=1, source_target_pairs={{0,2},{1,15},{2,4},{3,1},{4,6},{5,3},{6,8},{7,5},{8,10},{9,7},{10,... | collective-permute-start | bytes 393224 | tf_op jit(solution)/shard_map/ppermute | solution.py:52
  20.9 9.0 %collective-permute-start.8 = (bf16[2,128,256]{2,1,0:T(8,128)(2,1)S(1)}, bf16[2,128,256]{2,1,0:T(8,128)(2,1)S(1)}, u32[]{:S(2)}, u32[]{:S(2)}) collective-permute-start(bf16[2,128,256]{2,1,0:T(8,128)(2,1)S(1)} %pad_maximum_fusion), channel_id=1, source_target_pairs={{0,14},{1,3},{2,0},{3,5},{4,2},{5,7},{6,4},{7,9},{8,6},{9,11},{10,... | collective-permute-start | bytes 393224 | tf_op jit(solution)/shard_map/ppermute | solution.py:52
  22.1 27.7 %collective-permute-start.3 = (bf16[256,1536]{1,0:T(8,128)(2,1)S(1)}, bf16[256,1536]{1,0:T(8,128)(2,1)S(1)}, u32[]{:S(2)}, u32[]{:S(2)}) collective-permute-start(bf16[256,1536]{1,0:T(8,128)(2,1)S(1)} %collective-permute-done.2.h0), channel_id=1, source_target_pairs={{0,32},{1,97},{2,34},{3,99},{4,36},{5,101},{6,38},{7,103},{8,40},{... | collective-permute-start | bytes 2359304 | tf_op jit(solution)/shard_map/ppermute | solution.py:52
  22.7 27.1 %collective-permute-start.4 = (bf16[256,1536]{1,0:T(8,128)(2,1)S(1)}, bf16[256,1536]{1,0:T(8,128)(2,1)S(1)}, u32[]{:S(2)}, u32[]{:S(2)}) collective-permute-start(bf16[256,1536]{1,0:T(8,128)(2,1)S(1)} %collective-permute-done.2.h0), channel_id=1, source_target_pairs={{0,96},{1,33},{2,98},{3,35},{4,100},{5,37},{6,102},{7,39},{8,104},... | collective-permute-start | bytes 2359304 | tf_op jit(solution)/shard_map/ppermute | solution.py:52
  27.3 8.5 %collective-permute-start.9 = (bf16[2,128,256]{2,1,0:T(8,128)(2,1)S(1)}, bf16[2,128,256]{2,1,0:T(8,128)(2,1)S(1)}, u32[]{:S(2)}, u32[]{:S(2)}) collective-permute-start(bf16[2,128,256]{2,1,0:T(8,128)(2,1)S(1)} %pad_maximum_fusion), channel_id=1, source_target_pairs={{0,4},{1,13},{2,6},{3,15},{4,8},{5,1},{6,10},{7,3},{8,12},{9,5},{1... | collective-permute-start | bytes 393224 | tf_op jit(solution)/shard_map/ppermute | solution.py:52
  35.8 13.9 %collective-permute-start.10 = (bf16[8,128,256]{2,1,0:T(8,128)(2,1)S(1)}, bf16[8,128,256]{2,1,0:T(8,128)(2,1)S(1)}, u32[]{:S(2)}, u32[]{:S(2)}) collective-permute-start(bf16[8,128,256]{2,1,0:T(8,128)(2,1)S(1)} %constant_dynamic-update-slice_fusion.rest_0_), channel_id=1, source_target_pairs={{0,16},{1,145},{2,18},{3,147},{4,20},{5,149},{6,22},{7,151},{8,24}... | collective-permute-start | bytes 1572872 | tf_op jit(solution)/shard_map/ppermute | solution.py:52
  36.6 13.1 %collective-permute-start.11 = (bf16[8,128,256]{2,1,0:T(8,128)(2,1)S(1)}, bf16[8,128,256]{2,1,0:T(8,128)(2,1)S(1)}, u32[]{:S(2)}, u32[]{:S(2)}) collective-permute-start(bf16[8,128,256]{2,1,0:T(8,128)(2,1)S(1)} %constant_dynamic-update-slice_fusion.rest_0_), channel_id=1, source_target_pairs={{0,144},{1,17},{2,146},{3,19},{4,148},{5,21},{6,150},{7,23},{8,152... | collective-permute-start | bytes 1572872 | tf_op jit(solution)/shard_map/ppermute | solution.py:52
  39.2 1.9 %collective-permute-start.12 = (bf16[1536,128]{1,0:T(8,128)(2,1)}, bf16[1536,128]{1,0:T(8,128)(2,1)S(1)}, u32[]{:S(2)}, u32[]{:S(2)}) collective-permute-start(bf16[1536,128]{1,0:T(8,128)(2,1)} %pair.1), channel_id=1, source_target_pairs={{0,1},{1,0},{2,3},{3,2},{4,5},{5,4},{6,7},{7,6},{8,9},{9,8},{10,11... | collective-permute-start | bytes 1179656 | tf_op jit(solution)/shard_map/ppermute | solution.py:52
  41.1 10.1 %collective-permute-start.16 = (bf16[256,1536]{1,0:T(8,128)(2,1)S(1)}, bf16[256,1536]{1,0:T(8,128)(2,1)S(1)}, u32[]{:S(2)}, u32[]{:S(2)}) collective-permute-start(bf16[256,1536]{1,0:T(8,128)(2,1)S(1)} %collective-permute-done.2.h0), channel_id=1, source_target_pairs={{0,1},{1,0},{2,3},{3,2},{4,5},{5,4},{6,7},{7,6},{8,9},{9,8},{10,11... | collective-permute-start | bytes 2359304 | tf_op jit(solution)/shard_map/ppermute | solution.py:52
  49.7 4.9 %collective-permute-start.17 = (bf16[256,1536]{1,0:T(8,128)(2,1)S(1)}, bf16[256,1536]{1,0:T(8,128)(2,1)S(1)}, u32[]{:S(2)}, u32[]{:S(2)}) collective-permute-start(bf16[256,1536]{1,0:T(8,128)(2,1)S(1)} %collective-permute-done.3.h1), channel_id=1, source_target_pairs={{0,1},{1,0},{2,3},{3,2},{4,5},{5,4},{6,7},{7,6},{8,9},{9,8},{10,11... | collective-permute-start | bytes 2359304 | tf_op jit(solution)/shard_map/ppermute | solution.py:52
  49.8 4.8 %collective-permute-start.18 = (bf16[256,1536]{1,0:T(8,128)(2,1)S(1)}, bf16[256,1536]{1,0:T(8,128)(2,1)S(1)}, u32[]{:S(2)}, u32[]{:S(2)}) collective-permute-start(bf16[256,1536]{1,0:T(8,128)(2,1)S(1)} %collective-permute-done.4.h2), channel_id=1, source_target_pairs={{0,1},{1,0},{2,3},{3,2},{4,5},{5,4},{6,7},{7,6},{8,9},{9,8},{10,11... | collective-permute-start | bytes 2359304 | tf_op jit(solution)/shard_map/ppermute | solution.py:52
  50.3 13.2 %collective-permute-start.13 = (bf16[256,1536]{1,0:T(8,128)(2,1)S(1)}, bf16[256,1536]{1,0:T(8,128)(2,1)S(1)}, u32[]{:S(2)}, u32[]{:S(2)}) collective-permute-start(bf16[256,1536]{1,0:T(8,128)(2,1)S(1)} %collective-permute-done.3.h1), channel_id=1, source_target_pairs={{0,32},{1,97},{2,34},{3,99},{4,36},{5,101},{6,38},{7,103},{8,40},{... | collective-permute-start | bytes 2359304 | tf_op jit(solution)/shard_map/ppermute | solution.py:52
  51.1 9.0 %collective-permute-start.14 = (bf16[4,128,256]{2,1,0:T(8,128)(2,1)S(1)}, bf16[4,128,256]{2,1,0:T(8,128)(2,1)S(1)}, u32[]{:S(2)}, u32[]{:S(2)}) collective-permute-start(bf16[4,128,256]{2,1,0:T(8,128)(2,1)S(1)} %slice.26), channel_id=1, source_target_pairs={{0,16},{1,145},{2,18},{3,147},{4,20},{5,149},{6,22},{7,151},{8,24}... | collective-permute-start | bytes 786440 | tf_op jit(solution)/shard_map/ppermute | solution.py:52
  51.2 14.7 %copy-start = (bf16[1536,128]{1,0:T(8,128)(2,1)S(1)}, bf16[1536,128]{1,0:T(8,128)(2,1)}, u32[]{:S(2)}) copy-start(bf16[1536,128]{1,0:T(8,128)(2,1)} %pair.1) | copy-start | bytes 1179652
  51.2 8.8 %collective-permute-start.15 = (bf16[4,128,256]{2,1,0:T(8,128)(2,1)S(1)}, bf16[4,128,256]{2,1,0:T(8,128)(2,1)S(1)}, u32[]{:S(2)}, u32[]{:S(2)}) collective-permute-start(bf16[4,128,256]{2,1,0:T(8,128)(2,1)S(1)} %slice.27), channel_id=1, source_target_pairs={{0,144},{1,17},{2,146},{3,19},{4,148},{5,21},{6,150},{7,23},{8,152... | collective-permute-start | bytes 786440 | tf_op jit(solution)/shard_map/ppermute | solution.py:52
  63.5 2.3 %collective-permute-start.19 = (bf16[256,1536]{1,0:T(8,128)(2,1)S(1)}, bf16[256,1536]{1,0:T(8,128)(2,1)S(1)}, u32[]{:S(2)}, u32[]{:S(2)}) collective-permute-start(bf16[256,1536]{1,0:T(8,128)(2,1)S(1)} %collective-permute-done.13.h3), channel_id=1, source_target_pairs={{0,1},{1,0},{2,3},{3,2},{4,5},{5,4},{6,7},{7,6},{8,9},{9,8},{10,11... | collective-permute-start | bytes 2359304 | tf_op jit(solution)/shard_map/ppermute | solution.py:52

commit v4 on v3

--- a/solution.py
+++ b/solution.py
@@ -163,18 +163,19 @@
     *got, h0 = lax.optimization_barrier((*got, h0))
     parts = [(a[:64], send(a, CORE)[64:]) for a in got]
     block = jnp.stack([jnp.where(c == 0, jnp.concatenate([a, b]), jnp.concatenate([b, a])) for a, b in parts])
-    ring = jnp.concatenate([block, send(block, z_step(1)), send(block, z_step(-1)), send(block, z_step(2))])
+    z1, z2, z3 = (send(block, z_step(d)) for d in (1, -1, 2))
+    ring = jnp.concatenate([block, z1, z2, z3])
 
-    h1, h2 = send(h0, x_step(1)), send(h0, x_step(-1))
+    h1, h2 = send(h0, x_step(1)), send(lax.optimization_barrier((h0, z1))[0], x_step(-1))
     y1, y2 = send(ring, y_step(1)), send(ring, y_step(-1))
-    h1, h2, y1, y2, cspair = lax.optimization_barrier((h1, h2, y1, y2, cspair))
-    h3 = send(h1, x_step(1))
+    h3 = send(lax.optimization_barrier((h1, ring))[0], x_step(1))
+    h2, y1, y2, cspair = lax.optimization_barrier((h2, y1, y2, cspair))
     y3, y4 = send(y1[:4], y_step(1)), send(y2[4:], y_step(-1))
     h = [h0, h1, h2]
     g = [send(a, CORE) for a in h]
     shapes = ((512, 1536), jnp.float32), ((4, 8, 128, 256), jnp.bfloat16)
     gram, blocks = call(first_kernel, shapes, [], 1_800_000_000, *h, *g, ring, y1, y2)
-    h3, y3, y4, gram = lax.optimization_barrier((h3, y3, y4, gram))
+    y3, y4, gram = lax.optimization_barrier((y3, y4, gram))
     h.append(h3)
     g.append(send(h3, CORE))
     shapes = (((512, 128), jnp.float32),)

time: 88.3 us -> 84.1 us (0.952)
  waiting for transfers between devices: 29.3 us -> 22 us
  starting transfers between devices: 32.7 us -> 35.4 us
    ppermute x20, waiting for transfers between devices: 29.3 us -> 22 us  [send(): return lax.ppermute(a, AXES, perm)]
    ppermute x20, starting transfers between devices: 32.7 us -> 35.4 us  [send(): return lax.ppermute(a, AXES, perm)]
where the time goes in v4:
time: 84.1 us; the launch traced here: 83.9 us
  starting transfers between devices  35.4 us (42%)
  waiting for transfers between devices  22 us (26%)
  blocking collectives  19.2 us (23%)
  Pallas kernels  5.34 us (6%)
  matrix products  1.05 us (1%)
    ppermute x20, starting transfers between devices, send(): return lax.ppermute(a, AXES, perm)  35.4 us
    ppermute x20, waiting for transfers between devices, send(): return lax.ppermute(a, AXES, perm)  22 us
    all_to_all x1, blocking collectives, on_device(): parts = lax.all_to_all(part.reshape(32, 16, 128), ('yh', 'yl', 'z'), 0, 0)  19.2 us
    pallas_call x2, Pallas kernels, call(): pl.pallas_call(kernel, out_shape=[jax.ShapeDtypeStruct(*shape) for shape...  5.34 us
  transfers between devices with their start and end apart: 20, of which 9 were waited for; matrix products, arithmetic and copies ran while one was open for 1% of the time, Pallas kernels for 3%

profile of v4, /device:TPU:32, one launch (start us, length us, event | category | flops | bytes accessed | tf_op | source)
XLA Modules:
  0.0 83.9 jit_solution(16511543214206614216)
XLA Ops:
  0.0 1.8 %collective-permute-start.2 = (bf16[256,1536]{1,0:T(8,128)(2,1)}, bf16[256,1536]{1,0:T(8,128)(2,1)S(1)}, u32[]{:S(2)}, u32[]{:S(2)}) collective-permute-start(bf16[256,1536]{1,0:T(8,128)(2,1)} %param.3), channel_id=1, source_target_pairs={{0,0},{1,128},{2,2},{3,130},{4,4},{5,132},{6,6},{7,134},{8,8},{9,1... | collective-permute-start | bytes 2359304 | tf_op jit(solution)/shard_map/ppermute | solution.py:52
  1.8 1.0 %convolution_convert_fusion = bf16[128,256]{1,0:T(8,128)(2,1)S(1)} fusion(bf16[256,1536]{1,0:T(8,128)(2,1)} %param.3, bf16[2,128,128]{2,1,0:T(8,128)(2,1)} %constant.15.clone, s32[]{:T(128)S(6)} %select_n.30), kind=kOutput, calls=%fused_computation | convolution fusion | flops 8421376 | bytes 163844 | tf_op jit(solution)/shard_map/dot_general | solution.py:157
  2.8 0.7 collective-permute-start
  3.5 9.7 %collective-permute-start.1 = (bf16[128,256]{1,0:T(8,128)(2,1)S(1)}, bf16[128,256]{1,0:T(8,128)(2,1)S(1)}, u32[]{:S(2)}, u32[]{:S(2)}) collective-permute-start(bf16[128,256]{1,0:T(8,128)(2,1)S(1)} %convolution_convert_fusion), channel_id=1, source_target_pairs={{0,8},{1,9},{2,10},{3,11},{4,40},{5,41},{6,42},{7,43},{8,72},{9,73... | collective-permute-start | bytes 196616 | tf_op jit(solution)/shard_map/ppermute | solution.py:52
  13.2 0.0 collective-permute-done
  13.2 3.1 %collective-permute-done.1 = bf16[128,256]{1,0:T(8,128)(2,1)S(1)} collective-permute-done((bf16[128,256]{1,0:T(8,128)(2,1)S(1)}, bf16[128,256]{1,0:T(8,128)(2,1)S(1)}, u32[]{:S(2)}, u32[]{:S(2)}) %collective-permute-start.1) | collective-permute-done | bytes 65568 | tf_op jit(solution)/shard_map/ppermute | solution.py:52
  16.3 2.3 %collective-permute-start.3 = (bf16[128,256]{1,0:T(8,128)(2,1)S(1)}, bf16[128,256]{1,0:T(8,128)(2,1)S(1)}, u32[]{:S(2)}, u32[]{:S(2)}) collective-permute-start(bf16[128,256]{1,0:T(8,128)(2,1)S(1)} %collective-permute-done), channel_id=1, source_target_pairs={{0,1},{1,0},{2,3},{3,2},{4,5},{5,4},{6,7},{7,6},{8,9},{9,8},{10,11... | collective-permute-start | bytes 196616 | tf_op jit(solution)/shard_map/ppermute | solution.py:52
  18.7 0.1 collective-permute-start.4
  18.8 0.1 collective-permute-start.14
  18.8 0.7 collective-permute-done.3
  19.6 0.4 collective-permute-done.4
  20.0 1.6 %collective-permute-start.5 = (bf16[2,128,256]{2,1,0:T(8,128)(2,1)S(1)}, bf16[2,128,256]{2,1,0:T(8,128)(2,1)S(1)}, u32[]{:S(2)}, u32[]{:S(2)}) collective-permute-start(bf16[2,128,256]{2,1,0:T(8,128)(2,1)S(1)} %pad_maximum_fusion), channel_id=1, source_target_pairs={{0,2},{1,15},{2,4},{3,1},{4,6},{5,3},{6,8},{7,5},{8,10},{9,7},{10,... | collective-permute-start | bytes 393224 | tf_op jit(solution)/shard_map/ppermute | solution.py:52
  21.5 0.5 collective-permute-start.7
  22.1 3.9 %collective-permute-start.8 = (bf16[2,128,256]{2,1,0:T(8,128)(2,1)S(1)}, bf16[2,128,256]{2,1,0:T(8,128)(2,1)S(1)}, u32[]{:S(2)}, u32[]{:S(2)}) collective-permute-start(bf16[2,128,256]{2,1,0:T(8,128)(2,1)S(1)} %pad_maximum_fusion), channel_id=1, source_target_pairs={{0,4},{1,13},{2,6},{3,15},{4,8},{5,1},{6,10},{7,3},{8,12},{9,5},{1... | collective-permute-start | bytes 393224 | tf_op jit(solution)/shard_map/ppermute | solution.py:52
  26.0 5.4 %collective-permute-start.6 = (bf16[256,1536]{1,0:T(8,128)(2,1)S(1)}, bf16[256,1536]{1,0:T(8,128)(2,1)S(1)}, u32[]{:S(2)}, u32[]{:S(2)}) collective-permute-start(bf16[256,1536]{1,0:T(8,128)(2,1)S(1)} %collective-permute-done.2.h0), channel_id=1, source_target_pairs={{0,96},{1,33},{2,98},{3,35},{4,100},{5,37},{6,102},{7,39},{8,104},... | collective-permute-start | bytes 2359304 | tf_op jit(solution)/shard_map/ppermute | solution.py:52
  31.5 3.3 %collective-permute-done.14.h1 = bf16[256,1536]{1,0:T(8,128)(2,1)S(1)} collective-permute-done((bf16[256,1536]{1,0:T(8,128)(2,1)S(1)}, bf16[256,1536]{1,0:T(8,128)(2,1)S(1)}, u32[]{:S(2)}, u32[]{:S(2)}) %collective-permute-start.14) | collective-permute-done | bytes 786464 | tf_op jit(solution)/shard_map/ppermute | solution.py:52
  34.8 2.8 %collective-permute-start.18 = (bf16[256,1536]{1,0:T(8,128)(2,1)S(1)}, bf16[256,1536]{1,0:T(8,128)(2,1)S(1)}, u32[]{:S(2)}, u32[]{:S(2)}) collective-permute-start(bf16[256,1536]{1,0:T(8,128)(2,1)S(1)} %collective-permute-done.14.h1), channel_id=1, source_target_pairs={{0,32},{1,97},{2,34},{3,99},{4,36},{5,101},{6,38},{7,103},{8,40},{... | collective-permute-start | bytes 2359304 | tf_op jit(solution)/shard_map/ppermute | solution.py:52
  37.6 2.3 %collective-permute-start.10 = (bf16[8,128,256]{2,1,0:T(8,128)(2,1)S(1)}, bf16[8,128,256]{2,1,0:T(8,128)(2,1)S(1)}, u32[]{:S(2)}, u32[]{:S(2)}) collective-permute-start(bf16[8,128,256]{2,1,0:T(8,128)(2,1)S(1)} %constant_dynamic-update-slice_fusion.rest_0_), channel_id=1, source_target_pairs={{0,144},{1,17},{2,146},{3,19},{4,148},{5,21},{6,150},{7,23},{8,152... | collective-permute-start | bytes 1572872 | tf_op jit(solution)/shard_map/ppermute | solution.py:52
  39.9 1.9 %collective-permute-done.11.cspair = bf16[1536,128]{1,0:T(8,128)(2,1)S(1)} collective-permute-done((bf16[1536,128]{1,0:T(8,128)(2,1)}, bf16[1536,128]{1,0:T(8,128)(2,1)S(1)}, u32[]{:S(2)}, u32[]{:S(2)}) %collective-permute-start.11) | collective-permute-done | bytes 393248 | tf_op jit(solution)/shard_map/ppermute | solution.py:52
  41.8 0.1 collective-permute-start.15
  42.0 8.7 %collective-permute-done.10.rest_2_ = bf16[8,128,256]{2,1,0:T(8,128)(2,1)S(1)} collective-permute-done((bf16[8,128,256]{2,1,0:T(8,128)(2,1)S(1)}, bf16[8,128,256]{2,1,0:T(8,128)(2,1)S(1)}, u32[]{:S(2)}, u32[]{:S(2)}) %collective-permute-start.10) | collective-permute-done | bytes 524320 | tf_op jit(solution)/shard_map/ppermute | solution.py:52
  50.7 0.6 collective-permute-done.9.rest_1_
  51.4 0.5 collective-permute-start.19
  51.9 0.3 collective-permute-start.12
  52.2 0.0 copy-start
  52.2 3.3 %collective-permute-start.13 = (bf16[4,128,256]{2,1,0:T(8,128)(2,1)S(1)}, bf16[4,128,256]{2,1,0:T(8,128)(2,1)S(1)}, u32[]{:S(2)}, u32[]{:S(2)}) collective-permute-start(bf16[4,128,256]{2,1,0:T(8,128)(2,1)S(1)} %slice.27), channel_id=1, source_target_pairs={{0,144},{1,17},{2,146},{3,19},{4,148},{5,21},{6,150},{7,23},{8,152... | collective-permute-start | bytes 786440 | tf_op jit(solution)/shard_map/ppermute | solution.py:52
  55.5 2.5 %shard_map.37 = (f32[512,1536]{1,0:T(8,128)S(1)}, bf16[4,8,128,256]{3,2,1,0:T(8,128)(2,1)S(1)}) custom-call(bf16[256,1536]{1,0:T(8,128)(2,1)S(1)} %collective-permute-done.2.h0, bf16[256,1536]{1,0:T(8,128)(2,1)S(1)} %collective-permute-done.14.h1, bf16[256,1536]{1,0:T(8,128)(2,1)S(1)} %collective-permute-done.6.h2, ...), custom_call_target="tpu_custom_call" | custom-call | flops 1800000000 | bytes 9000000 | tf_op jit(solution)/shard_map/pallas_call | solution.py:142
  58.0 1.8 %collective-permute-done.12.y3 = bf16[4,128,256]{2,1,0:T(8,128)(2,1)S(1)} collective-permute-done((bf16[4,128,256]{2,1,0:T(8,128)(2,1)S(1)}, bf16[4,128,256]{2,1,0:T(8,128)(2,1)S(1)}, u32[]{:S(2)}, u32[]{:S(2)}) %collective-permute-start.12) | collective-permute-done | bytes 262176 | tf_op jit(solution)/shard_map/ppermute | solution.py:52
  59.8 1.4 %collective-permute-done.13.y4 = bf16[4,128,256]{2,1,0:T(8,128)(2,1)S(1)} collective-permute-done((bf16[4,128,256]{2,1,0:T(8,128)(2,1)S(1)}, bf16[4,128,256]{2,1,0:T(8,128)(2,1)S(1)}, u32[]{:S(2)}, u32[]{:S(2)}) %collective-permute-start.13) | collective-permute-done | bytes 262176 | tf_op jit(solution)/shard_map/ppermute | solution.py:52
  61.2 2.9 %shard_map.38 = f32[512,128]{1,0:T(8,128)S(1)} custom-call(f32[512,1536]{1,0:T(8,128)S(1)} %get-tuple-element.27.gram, bf16[4,8,128,256]{3,2,1,0:T(8,128)(2,1)S(1)} %get-tuple-element.28.blocks, bf16[256,1536]{1,0:T(8,128)(2,1)S(1)} %collective-permute-done.2.h0, bf16[256,1536]{1,0:T(8,128)(2,1)S(1)} %collective-permute-done.14.h1, ...), custom_call_target="tpu_custom_call" | custom-call | flops 1600000000 | bytes 9000000 | tf_op jit(solution)/shard_map/pallas_call | solution.py:142
  64.1 19.2 %all_to_all.5 = f32[32,16,128]{2,1,0:T(8,128)S(1)} all-to-all(f32[32,16,128]{2,1,0:T(8,128)S(1)} %bitcast.12), channel_id=1, replica_groups=mesh['yh'=2,'x'=4,'yl'=2,'z'=8,'c'=2] {'yh','yl','z'}, dimensions={0} | all-to-all | bytes 524288 | tf_op jit(solution)/shard_map/all_to_all | solution.py:184
  83.3 0.6 reduce_sum.9
  (26 shorter events, 0.2 us)
Async XLA Ops:
  0.0 16.3 %collective-permute-start.2 = (bf16[256,1536]{1,0:T(8,128)(2,1)}, bf16[256,1536]{1,0:T(8,128)(2,1)S(1)}, u32[]{:S(2)}, u32[]{:S(2)}) collective-permute-start(bf16[256,1536]{1,0:T(8,128)(2,1)} %param.3), channel_id=1, source_target_pairs={{0,0},{1,128},{2,2},{3,130},{4,4},{5,132},{6,6},{7,134},{8,8},{9,1... | collective-permute-start | bytes 2359304 | tf_op jit(solution)/shard_map/ppermute | solution.py:52
  2.8 10.4 %collective-permute-start = (bf16[128,256]{1,0:T(8,128)(2,1)S(1)}, bf16[128,256]{1,0:T(8,128)(2,1)S(1)}, u32[]{:S(2)}, u32[]{:S(2)}) collective-permute-start(bf16[128,256]{1,0:T(8,128)(2,1)S(1)} %convolution_convert_fusion), channel_id=1, source_target_pairs={{0,0},{1,1},{2,2},{3,3},{4,32},{5,33},{6,34},{7,35},{8,64},{9,65},... | collective-permute-start | bytes 196616 | tf_op jit(solution)/shard_map/ppermute | solution.py:52
  3.5 12.8 %collective-permute-start.1 = (bf16[128,256]{1,0:T(8,128)(2,1)S(1)}, bf16[128,256]{1,0:T(8,128)(2,1)S(1)}, u32[]{:S(2)}, u32[]{:S(2)}) collective-permute-start(bf16[128,256]{1,0:T(8,128)(2,1)S(1)} %convolution_convert_fusion), channel_id=1, source_target_pairs={{0,8},{1,9},{2,10},{3,11},{4,40},{5,41},{6,42},{7,43},{8,72},{9,73... | collective-permute-start | bytes 196616 | tf_op jit(solution)/shard_map/ppermute | solution.py:52
  16.3 3.2 %collective-permute-start.3 = (bf16[128,256]{1,0:T(8,128)(2,1)S(1)}, bf16[128,256]{1,0:T(8,128)(2,1)S(1)}, u32[]{:S(2)}, u32[]{:S(2)}) collective-permute-start(bf16[128,256]{1,0:T(8,128)(2,1)S(1)} %collective-permute-done), channel_id=1, source_target_pairs={{0,1},{1,0},{2,3},{3,2},{4,5},{5,4},{6,7},{7,6},{8,9},{9,8},{10,11... | collective-permute-start | bytes 196616 | tf_op jit(solution)/shard_map/ppermute | solution.py:52
  18.7 1.3 %collective-permute-start.4 = (bf16[128,256]{1,0:T(8,128)(2,1)S(1)}, bf16[128,256]{1,0:T(8,128)(2,1)S(1)}, u32[]{:S(2)}, u32[]{:S(2)}) collective-permute-start(bf16[128,256]{1,0:T(8,128)(2,1)S(1)} %collective-permute-done.1), channel_id=1, source_target_pairs={{0,1},{1,0},{2,3},{3,2},{4,5},{5,4},{6,7},{7,6},{8,9},{9,8},{10,11... | collective-permute-start | bytes 196616 | tf_op jit(solution)/shard_map/ppermute | solution.py:52
  18.8 16.0 %collective-permute-start.14 = (bf16[256,1536]{1,0:T(8,128)(2,1)S(1)}, bf16[256,1536]{1,0:T(8,128)(2,1)S(1)}, u32[]{:S(2)}, u32[]{:S(2)}) collective-permute-start(bf16[256,1536]{1,0:T(8,128)(2,1)S(1)} %collective-permute-done.2.h0), channel_id=1, source_target_pairs={{0,32},{1,97},{2,34},{3,99},{4,36},{5,101},{6,38},{7,103},{8,40},{... | collective-permute-start | bytes 2359304 | tf_op jit(solution)/shard_map/ppermute | solution.py:52
  20.0 6.0 %collective-permute-start.5 = (bf16[2,128,256]{2,1,0:T(8,128)(2,1)S(1)}, bf16[2,128,256]{2,1,0:T(8,128)(2,1)S(1)}, u32[]{:S(2)}, u32[]{:S(2)}) collective-permute-start(bf16[2,128,256]{2,1,0:T(8,128)(2,1)S(1)} %pad_maximum_fusion), channel_id=1, source_target_pairs={{0,2},{1,15},{2,4},{3,1},{4,6},{5,3},{6,8},{7,5},{8,10},{9,7},{10,... | collective-permute-start | bytes 393224 | tf_op jit(solution)/shard_map/ppermute | solution.py:52
  21.5 9.9 %collective-permute-start.7 = (bf16[2,128,256]{2,1,0:T(8,128)(2,1)S(1)}, bf16[2,128,256]{2,1,0:T(8,128)(2,1)S(1)}, u32[]{:S(2)}, u32[]{:S(2)}) collective-permute-start(bf16[2,128,256]{2,1,0:T(8,128)(2,1)S(1)} %pad_maximum_fusion), channel_id=1, source_target_pairs={{0,14},{1,3},{2,0},{3,5},{4,2},{5,7},{6,4},{7,9},{8,6},{9,11},{10,... | collective-permute-start | bytes 393224 | tf_op jit(solution)/shard_map/ppermute | solution.py:52
  22.1 9.4 %collective-permute-start.8 = (bf16[2,128,256]{2,1,0:T(8,128)(2,1)S(1)}, bf16[2,128,256]{2,1,0:T(8,128)(2,1)S(1)}, u32[]{:S(2)}, u32[]{:S(2)}) collective-permute-start(bf16[2,128,256]{2,1,0:T(8,128)(2,1)S(1)} %pad_maximum_fusion), channel_id=1, source_target_pairs={{0,4},{1,13},{2,6},{3,15},{4,8},{5,1},{6,10},{7,3},{8,12},{9,5},{1... | collective-permute-start | bytes 393224 | tf_op jit(solution)/shard_map/ppermute | solution.py:52
  26.0 25.4 %collective-permute-start.6 = (bf16[256,1536]{1,0:T(8,128)(2,1)S(1)}, bf16[256,1536]{1,0:T(8,128)(2,1)S(1)}, u32[]{:S(2)}, u32[]{:S(2)}) collective-permute-start(bf16[256,1536]{1,0:T(8,128)(2,1)S(1)} %collective-permute-done.2.h0), channel_id=1, source_target_pairs={{0,96},{1,33},{2,98},{3,35},{4,100},{5,37},{6,102},{7,39},{8,104},... | collective-permute-start | bytes 2359304 | tf_op jit(solution)/shard_map/ppermute | solution.py:52
  34.8 16.6 %collective-permute-start.18 = (bf16[256,1536]{1,0:T(8,128)(2,1)S(1)}, bf16[256,1536]{1,0:T(8,128)(2,1)S(1)}, u32[]{:S(2)}, u32[]{:S(2)}) collective-permute-start(bf16[256,1536]{1,0:T(8,128)(2,1)S(1)} %collective-permute-done.14.h1), channel_id=1, source_target_pairs={{0,32},{1,97},{2,34},{3,99},{4,36},{5,101},{6,38},{7,103},{8,40},{... | collective-permute-start | bytes 2359304 | tf_op jit(solution)/shard_map/ppermute | solution.py:52
  37.6 13.1 %collective-permute-start.10 = (bf16[8,128,256]{2,1,0:T(8,128)(2,1)S(1)}, bf16[8,128,256]{2,1,0:T(8,128)(2,1)S(1)}, u32[]{:S(2)}, u32[]{:S(2)}) collective-permute-start(bf16[8,128,256]{2,1,0:T(8,128)(2,1)S(1)} %constant_dynamic-update-slice_fusion.rest_0_), channel_id=1, source_target_pairs={{0,144},{1,17},{2,146},{3,19},{4,148},{5,21},{6,150},{7,23},{8,152... | collective-permute-start | bytes 1572872 | tf_op jit(solution)/shard_map/ppermute | solution.py:52
  39.9 11.5 %collective-permute-start.9 = (bf16[8,128,256]{2,1,0:T(8,128)(2,1)S(1)}, bf16[8,128,256]{2,1,0:T(8,128)(2,1)S(1)}, u32[]{:S(2)}, u32[]{:S(2)}) collective-permute-start(bf16[8,128,256]{2,1,0:T(8,128)(2,1)S(1)} %constant_dynamic-update-slice_fusion.rest_0_), channel_id=1, source_target_pairs={{0,16},{1,145},{2,18},{3,147},{4,20},{5,149},{6,22},{7,151},{8,24}... | collective-permute-start | bytes 1572872 | tf_op jit(solution)/shard_map/ppermute | solution.py:52
  39.9 1.9 %collective-permute-start.11 = (bf16[1536,128]{1,0:T(8,128)(2,1)}, bf16[1536,128]{1,0:T(8,128)(2,1)S(1)}, u32[]{:S(2)}, u32[]{:S(2)}) collective-permute-start(bf16[1536,128]{1,0:T(8,128)(2,1)} %pair.1), channel_id=1, source_target_pairs={{0,1},{1,0},{2,3},{3,2},{4,5},{5,4},{6,7},{7,6},{8,9},{9,8},{10,11... | collective-permute-start | bytes 1179656 | tf_op jit(solution)/shard_map/ppermute | solution.py:52
  41.8 10.4 %collective-permute-start.15 = (bf16[256,1536]{1,0:T(8,128)(2,1)S(1)}, bf16[256,1536]{1,0:T(8,128)(2,1)S(1)}, u32[]{:S(2)}, u32[]{:S(2)}) collective-permute-start(bf16[256,1536]{1,0:T(8,128)(2,1)S(1)} %collective-permute-done.2.h0), channel_id=1, source_target_pairs={{0,1},{1,0},{2,3},{3,2},{4,5},{5,4},{6,7},{7,6},{8,9},{9,8},{10,11... | collective-permute-start | bytes 2359304 | tf_op jit(solution)/shard_map/ppermute | solution.py:52
  50.7 4.8 %collective-permute-start.16 = (bf16[256,1536]{1,0:T(8,128)(2,1)S(1)}, bf16[256,1536]{1,0:T(8,128)(2,1)S(1)}, u32[]{:S(2)}, u32[]{:S(2)}) collective-permute-start(bf16[256,1536]{1,0:T(8,128)(2,1)S(1)} %collective-permute-done.14.h1), channel_id=1, source_target_pairs={{0,1},{1,0},{2,3},{3,2},{4,5},{5,4},{6,7},{7,6},{8,9},{9,8},{10,11... | collective-permute-start | bytes 2359304 | tf_op jit(solution)/shard_map/ppermute | solution.py:52
  51.4 4.2 %collective-permute-start.17 = (bf16[256,1536]{1,0:T(8,128)(2,1)S(1)}, bf16[256,1536]{1,0:T(8,128)(2,1)S(1)}, u32[]{:S(2)}, u32[]{:S(2)}) collective-permute-start(bf16[256,1536]{1,0:T(8,128)(2,1)S(1)} %collective-permute-done.6.h2), channel_id=1, source_target_pairs={{0,1},{1,0},{2,3},{3,2},{4,5},{5,4},{6,7},{7,6},{8,9},{9,8},{10,11... | collective-permute-start | bytes 2359304 | tf_op jit(solution)/shard_map/ppermute | solution.py:52
  51.4 9.8 %collective-permute-start.19 = (bf16[256,1536]{1,0:T(8,128)(2,1)S(1)}, bf16[256,1536]{1,0:T(8,128)(2,1)S(1)}, u32[]{:S(2)}, u32[]{:S(2)}) collective-permute-start(bf16[256,1536]{1,0:T(8,128)(2,1)S(1)} %collective-permute-done.18.h3), channel_id=1, source_target_pairs={{0,1},{1,0},{2,3},{3,2},{4,5},{5,4},{6,7},{7,6},{8,9},{9,8},{10,11... | collective-permute-start | bytes 2359304 | tf_op jit(solution)/shard_map/ppermute | solution.py:52
  51.9 7.9 %collective-permute-start.12 = (bf16[4,128,256]{2,1,0:T(8,128)(2,1)S(1)}, bf16[4,128,256]{2,1,0:T(8,128)(2,1)S(1)}, u32[]{:S(2)}, u32[]{:S(2)}) collective-permute-start(bf16[4,128,256]{2,1,0:T(8,128)(2,1)S(1)} %slice.26), channel_id=1, source_target_pairs={{0,16},{1,145},{2,18},{3,147},{4,20},{5,149},{6,22},{7,151},{8,24}... | collective-permute-start | bytes 786440 | tf_op jit(solution)/shard_map/ppermute | solution.py:52
  52.2 9.0 %copy-start = (bf16[1536,128]{1,0:T(8,128)(2,1)S(1)}, bf16[1536,128]{1,0:T(8,128)(2,1)}, u32[]{:S(2)}) copy-start(bf16[1536,128]{1,0:T(8,128)(2,1)} %pair.1) | copy-start | bytes 1179652
  52.2 9.0 %collective-permute-start.13 = (bf16[4,128,256]{2,1,0:T(8,128)(2,1)S(1)}, bf16[4,128,256]{2,1,0:T(8,128)(2,1)S(1)}, u32[]{:S(2)}, u32[]{:S(2)}) collective-permute-start(bf16[4,128,256]{2,1,0:T(8,128)(2,1)S(1)} %slice.27), channel_id=1, source_target_pairs={{0,144},{1,17},{2,146},{3,19},{4,148},{5,21},{6,150},{7,23},{8,152... | collective-permute-start | bytes 786440 | tf_op jit(solution)/shard_map/ppermute | solution.py:52

commit v5 on v4

--- a/solution.py
+++ b/solution.py
@@ -33,7 +33,7 @@
 
 CORE = perm_of(lambda x, y, z, c: (x, y, z, 1 - c))
 SPREAD, SPREAD_FAR = (perm_of(lambda x, y, z, c: (z // 2, y, 2 * x + z % 2 + d, c)) for d in (0, 4))
-TRADE = perm_of(lambda x, y, z, c: (x, y, z, c) if is_own(y, c) else (x, y + 2, z, 1 - c))
+TRADE = perm_of(lambda x, y, z, c: (x, y + 2, z, 1 - c), lambda yh, c: c != yh)
 
 
 def x_step(d):
@@ -161,6 +161,7 @@
     h0 = send(collocation, TRADE)
     cspair = send(pair_tensor, CORE)
     *got, h0 = lax.optimization_barrier((*got, h0))
+    h0 = jnp.where(c == lax.axis_index("yh"), collocation, h0)
     parts = [(a[:64], send(a, CORE)[64:]) for a in got]
     block = jnp.stack([jnp.where(c == 0, jnp.concatenate([a, b]), jnp.concatenate([b, a])) for a, b in parts])
     z1, z2, z3 = (send(block, z_step(d)) for d in (1, -1, 2))

time: 84.1 us -> 85.1 us (1.012)
  waiting for transfers between devices: 22 us -> 20.7 us
  other arithmetic: 0.68 us -> 1.9 us
    ppermute x20, waiting for transfers between devices: 22 us -> 20.7 us  [send(): return lax.ppermute(a, AXES, perm)]
    select_n x0 -> x1, other arithmetic: none -> 1.22 us  [on_device(): h0 = jnp.where(c == lax.axis_index('yh'), collocation, h0)]
  transfers between devices with their start and end apart: 20 -> 20, of which waited for: 9 -> 7; matrix products, arithmetic and copies ran while one was open for 1% -> 3% of each run, Pallas kernels for 3% -> 3%
where the time goes in v5:
time: 85.1 us; the launch traced here: 84.9 us
  starting transfers between devices  36.2 us (43%)
  waiting for transfers between devices  20.7 us (24%)
  blocking collectives  19.4 us (23%)
  Pallas kernels  5.34 us (6%)
  other arithmetic  1.9 us (2%)
  matrix products  1.06 us (1%)
    ppermute x20, starting transfers between devices, send(): return lax.ppermute(a, AXES, perm)  36.2 us
    ppermute x20, waiting for transfers between devices, send(): return lax.ppermute(a, AXES, perm)  20.7 us
    all_to_all x1, blocking collectives, on_device(): parts = lax.all_to_all(part.reshape(32, 16, 128), ('yh', 'yl', 'z'), 0, 0)  19.4 us
    pallas_call x2, Pallas kernels, call(): pl.pallas_call(kernel, out_shape=[jax.ShapeDtypeStruct(*shape) for shape...  5.34 us
  transfers between devices with their start and end apart: 20, of which 7 were waited for; matrix products, arithmetic and copies ran while one was open for 3% of the time, Pallas kernels for 3%

profile of v5, /device:TPU:32, one launch (start us, length us, event | category | flops | bytes accessed | tf_op | source)
XLA Modules:
  0.0 84.9 jit_solution(8288742971082769701)
XLA Ops:
  0.0 0.8 collective-permute-start.2
  0.8 1.1 %convolution_convert_fusion = bf16[128,256]{1,0:T(8,128)(2,1)S(1)} fusion(bf16[256,1536]{1,0:T(8,128)(2,1)} %param.3, bf16[2,128,128]{2,1,0:T(8,128)(2,1)} %constant.19.clone, s32[]{:T(128)S(6)} %select_n.39), kind=kOutput, calls=%fused_computation | convolution fusion | flops 8421376 | bytes 163844 | tf_op jit(solution)/shard_map/dot_general | solution.py:157
  1.9 0.7 collective-permute-start
  2.6 9.7 %collective-permute-start.1 = (bf16[128,256]{1,0:T(8,128)(2,1)S(1)}, bf16[128,256]{1,0:T(8,128)(2,1)S(1)}, u32[]{:S(2)}, u32[]{:S(2)}) collective-permute-start(bf16[128,256]{1,0:T(8,128)(2,1)S(1)} %convolution_convert_fusion), channel_id=1, source_target_pairs={{0,8},{1,9},{2,10},{3,11},{4,40},{5,41},{6,42},{7,43},{8,72},{9,73... | collective-permute-start | bytes 196616 | tf_op jit(solution)/shard_map/ppermute | solution.py:52
  12.3 3.1 %collective-permute-done.1 = bf16[128,256]{1,0:T(8,128)(2,1)S(1)} collective-permute-done((bf16[128,256]{1,0:T(8,128)(2,1)S(1)}, bf16[128,256]{1,0:T(8,128)(2,1)S(1)}, u32[]{:S(2)}, u32[]{:S(2)}) %collective-permute-start.1) | collective-permute-done | bytes 65568 | tf_op jit(solution)/shard_map/ppermute | solution.py:52
  15.4 0.0 collective-permute-done.2
  15.4 3.6 %collective-permute-start.3 = (bf16[128,256]{1,0:T(8,128)(2,1)S(1)}, bf16[128,256]{1,0:T(8,128)(2,1)S(1)}, u32[]{:S(2)}, u32[]{:S(2)}) collective-permute-start(bf16[128,256]{1,0:T(8,128)(2,1)S(1)} %collective-permute-done), channel_id=1, source_target_pairs={{0,1},{1,0},{2,3},{3,2},{4,5},{5,4},{6,7},{7,6},{8,9},{9,8},{10,11... | collective-permute-start | bytes 196616 | tf_op jit(solution)/shard_map/ppermute | solution.py:52
  19.1 0.1 collective-permute-start.4
  19.2 1.2 %broadcast_select_fusion.h0 = bf16[256,1536]{1,0:T(8,128)(2,1)S(1)} fusion(bf16[256,1536]{1,0:T(8,128)(2,1)} %param.3, bf16[256,1536]{1,0:T(8,128)(2,1)S(1)} %collective-permute-done.2, pred[]{:T(512)S(6)} %eq.7), kind=kLoop, calls=%fused_computation.1 | loop fusion | flops 393216 | bytes 2359297 | tf_op jit(solution)/shard_map/jit(_where)/select_n | solution.py:164
  20.4 0.1 collective-permute-start.14
  20.5 0.0 collective-permute-done.4
  20.6 2.3 %collective-permute-start.5 = (bf16[2,128,256]{2,1,0:T(8,128)(2,1)S(1)}, bf16[2,128,256]{2,1,0:T(8,128)(2,1)S(1)}, u32[]{:S(2)}, u32[]{:S(2)}) collective-permute-start(bf16[2,128,256]{2,1,0:T(8,128)(2,1)S(1)} %pad_maximum_fusion), channel_id=1, source_target_pairs={{0,2},{1,15},{2,4},{3,1},{4,6},{5,3},{6,8},{7,5},{8,10},{9,7},{10,... | collective-permute-start | bytes 393224 | tf_op jit(solution)/shard_map/ppermute | solution.py:52
  22.9 2.9 %collective-permute-start.8 = (bf16[2,128,256]{2,1,0:T(8,128)(2,1)S(1)}, bf16[2,128,256]{2,1,0:T(8,128)(2,1)S(1)}, u32[]{:S(2)}, u32[]{:S(2)}) collective-permute-start(bf16[2,128,256]{2,1,0:T(8,128)(2,1)S(1)} %pad_maximum_fusion), channel_id=1, source_target_pairs={{0,4},{1,13},{2,6},{3,15},{4,8},{5,1},{6,10},{7,3},{8,12},{9,5},{1... | collective-permute-start | bytes 393224 | tf_op jit(solution)/shard_map/ppermute | solution.py:52
  25.8 0.0 collective-permute-done.5
  25.8 4.9 %collective-permute-start.6 = (bf16[256,1536]{1,0:T(8,128)(2,1)S(1)}, bf16[256,1536]{1,0:T(8,128)(2,1)S(1)}, u32[]{:S(2)}, u32[]{:S(2)}) collective-permute-start(bf16[256,1536]{1,0:T(8,128)(2,1)S(1)} %broadcast_select_fusion.h0), channel_id=1, source_target_pairs={{0,96},{1,33},{2,98},{3,35},{4,100},{5,37},{6,102},{7,39},{8,104},... | collective-permute-start | bytes 2359304 | tf_op jit(solution)/shard_map/ppermute | solution.py:52
  30.7 1.7 %collective-permute-done.8 = bf16[2,128,256]{2,1,0:T(8,128)(2,1)S(1)} collective-permute-done((bf16[2,128,256]{2,1,0:T(8,128)(2,1)S(1)}, bf16[2,128,256]{2,1,0:T(8,128)(2,1)S(1)}, u32[]{:S(2)}, u32[]{:S(2)}) %collective-permute-start.8) | collective-permute-done | bytes 131104 | tf_op jit(solution)/shard_map/ppermute | solution.py:52
  32.4 3.2 %collective-permute-done.14.h1 = bf16[256,1536]{1,0:T(8,128)(2,1)S(1)} collective-permute-done((bf16[256,1536]{1,0:T(8,128)(2,1)S(1)}, bf16[256,1536]{1,0:T(8,128)(2,1)S(1)}, u32[]{:S(2)}, u32[]{:S(2)}) %collective-permute-start.14) | collective-permute-done | bytes 786464 | tf_op jit(solution)/shard_map/ppermute | solution.py:52
  35.6 4.7 %collective-permute-start.18 = (bf16[256,1536]{1,0:T(8,128)(2,1)S(1)}, bf16[256,1536]{1,0:T(8,128)(2,1)S(1)}, u32[]{:S(2)}, u32[]{:S(2)}) collective-permute-start(bf16[256,1536]{1,0:T(8,128)(2,1)S(1)} %collective-permute-done.14.h1), channel_id=1, source_target_pairs={{0,32},{1,97},{2,34},{3,99},{4,36},{5,101},{6,38},{7,103},{8,40},{... | collective-permute-start | bytes 2359304 | tf_op jit(solution)/shard_map/ppermute | solution.py:52
  40.3 2.0 %collective-permute-start.9 = (bf16[8,128,256]{2,1,0:T(8,128)(2,1)S(1)}, bf16[8,128,256]{2,1,0:T(8,128)(2,1)S(1)}, u32[]{:S(2)}, u32[]{:S(2)}) collective-permute-start(bf16[8,128,256]{2,1,0:T(8,128)(2,1)S(1)} %constant_dynamic-update-slice_fusion.rest_0_), channel_id=1, source_target_pairs={{0,16},{1,145},{2,18},{3,147},{4,20},{5,149},{6,22},{7,151},{8,24}... | collective-permute-start | bytes 1572872 | tf_op jit(solution)/shard_map/ppermute | solution.py:52
  42.4 1.7 %collective-permute-done.11.cspair = bf16[1536,128]{1,0:T(8,128)(2,1)S(1)} collective-permute-done((bf16[1536,128]{1,0:T(8,128)(2,1)S(1)}, bf16[1536,128]{1,0:T(8,128)(2,1)S(1)}, u32[]{:S(2)}, u32[]{:S(2)}) %collective-permute-start.11) | collective-permute-done | bytes 393248 | tf_op jit(solution)/shard_map/ppermute | solution.py:52
  44.1 0.1 collective-permute-start.15
  44.2 7.9 %collective-permute-done.10.rest_2_ = bf16[8,128,256]{2,1,0:T(8,128)(2,1)S(1)} collective-permute-done((bf16[8,128,256]{2,1,0:T(8,128)(2,1)S(1)}, bf16[8,128,256]{2,1,0:T(8,128)(2,1)S(1)}, u32[]{:S(2)}, u32[]{:S(2)}) %collective-permute-start.10) | collective-permute-done | bytes 524320 | tf_op jit(solution)/shard_map/ppermute | solution.py:52
  52.2 0.5 collective-permute-start.17
  52.7 0.1 collective-permute-start.19
  52.8 1.8 %collective-permute-start.12 = (bf16[4,128,256]{2,1,0:T(8,128)(2,1)S(1)}, bf16[4,128,256]{2,1,0:T(8,128)(2,1)S(1)}, u32[]{:S(2)}, u32[]{:S(2)}) collective-permute-start(bf16[4,128,256]{2,1,0:T(8,128)(2,1)S(1)} %slice.26), channel_id=1, source_target_pairs={{0,16},{1,145},{2,18},{3,147},{4,20},{5,149},{6,22},{7,151},{8,24}... | collective-permute-start | bytes 786440 | tf_op jit(solution)/shard_map/ppermute | solution.py:52
  54.7 1.8 %collective-permute-start.13 = (bf16[4,128,256]{2,1,0:T(8,128)(2,1)S(1)}, bf16[4,128,256]{2,1,0:T(8,128)(2,1)S(1)}, u32[]{:S(2)}, u32[]{:S(2)}) collective-permute-start(bf16[4,128,256]{2,1,0:T(8,128)(2,1)S(1)} %slice.27), channel_id=1, source_target_pairs={{0,144},{1,17},{2,146},{3,19},{4,148},{5,21},{6,150},{7,23},{8,152... | collective-permute-start | bytes 786440 | tf_op jit(solution)/shard_map/ppermute | solution.py:52
  56.4 2.5 %shard_map.37 = (f32[512,1536]{1,0:T(8,128)S(1)}, bf16[4,8,128,256]{3,2,1,0:T(8,128)(2,1)S(1)}) custom-call(bf16[256,1536]{1,0:T(8,128)(2,1)S(1)} %broadcast_select_fusion.h0, bf16[256,1536]{1,0:T(8,128)(2,1)S(1)} %collective-permute-done.14.h1, bf16[256,1536]{1,0:T(8,128)(2,1)S(1)} %collective-permute-done.6.h2, ...), custom_call_target="tpu_custom_call" | custom-call | flops 1800000000 | bytes 9000000 | tf_op jit(solution)/shard_map/pallas_call | solution.py:142
  58.9 1.9 %collective-permute-done.12.y3 = bf16[4,128,256]{2,1,0:T(8,128)(2,1)S(1)} collective-permute-done((bf16[4,128,256]{2,1,0:T(8,128)(2,1)S(1)}, bf16[4,128,256]{2,1,0:T(8,128)(2,1)S(1)}, u32[]{:S(2)}, u32[]{:S(2)}) %collective-permute-start.12) | collective-permute-done | bytes 262176 | tf_op jit(solution)/shard_map/ppermute | solution.py:52
  60.8 1.1 %collective-permute-done.13.y4 = bf16[4,128,256]{2,1,0:T(8,128)(2,1)S(1)} collective-permute-done((bf16[4,128,256]{2,1,0:T(8,128)(2,1)S(1)}, bf16[4,128,256]{2,1,0:T(8,128)(2,1)S(1)}, u32[]{:S(2)}, u32[]{:S(2)}) %collective-permute-start.13) | collective-permute-done | bytes 262176 | tf_op jit(solution)/shard_map/ppermute | solution.py:52
  62.0 2.9 %shard_map.38 = f32[512,128]{1,0:T(8,128)S(1)} custom-call(f32[512,1536]{1,0:T(8,128)S(1)} %get-tuple-element.27.gram, bf16[4,8,128,256]{3,2,1,0:T(8,128)(2,1)S(1)} %get-tuple-element.28.blocks, bf16[256,1536]{1,0:T(8,128)(2,1)S(1)} %broadcast_select_fusion.h0, bf16[256,1536]{1,0:T(8,128)(2,1)S(1)} %collective-permute-done.14.h1, ...), custom_call_target="tpu_custom_call" | custom-call | flops 1600000000 | bytes 9000000 | tf_op jit(solution)/shard_map/pallas_call | solution.py:142
  64.8 19.4 %all_to_all.5 = f32[32,16,128]{2,1,0:T(8,128)S(1)} all-to-all(f32[32,16,128]{2,1,0:T(8,128)S(1)} %bitcast.12), channel_id=1, replica_groups=mesh['yh'=2,'x'=4,'yl'=2,'z'=8,'c'=2] {'yh','yl','z'}, dimensions={0} | all-to-all | bytes 524288 | tf_op jit(solution)/shard_map/all_to_all | solution.py:185
  84.2 0.6 reduce_sum.9
  (27 shorter events, 0.2 us)
Async XLA Ops:
  0.0 42.4 %copy-start = (bf16[1536,128]{1,0:T(8,128)(2,1)S(1)}, bf16[1536,128]{1,0:T(8,128)(2,1)}, u32[]{:S(2)}) copy-start(bf16[1536,128]{1,0:T(8,128)(2,1)} %pair.1) | copy-start | bytes 1179652
  0.0 15.4 %collective-permute-start.2 = (bf16[256,1536]{1,0:T(8,128)(2,1)}, bf16[256,1536]{1,0:T(8,128)(2,1)S(1)}, u32[]{:S(2)}, u32[]{:S(2)}) collective-permute-start(bf16[256,1536]{1,0:T(8,128)(2,1)} %param.3), channel_id=1, source_target_pairs={{1,128},{3,130},{5,132},{7,134},{9,136},{11,138},{13,140},{15,142}... | collective-permute-start | bytes 2359304 | tf_op jit(solution)/shard_map/ppermute | solution.py:52
  1.9 10.4 %collective-permute-start = (bf16[128,256]{1,0:T(8,128)(2,1)S(1)}, bf16[128,256]{1,0:T(8,128)(2,1)S(1)}, u32[]{:S(2)}, u32[]{:S(2)}) collective-permute-start(bf16[128,256]{1,0:T(8,128)(2,1)S(1)} %convolution_convert_fusion), channel_id=1, source_target_pairs={{0,0},{1,1},{2,2},{3,3},{4,32},{5,33},{6,34},{7,35},{8,64},{9,65},... | collective-permute-start | bytes 196616 | tf_op jit(solution)/shard_map/ppermute | solution.py:52
  2.6 12.8 %collective-permute-start.1 = (bf16[128,256]{1,0:T(8,128)(2,1)S(1)}, bf16[128,256]{1,0:T(8,128)(2,1)S(1)}, u32[]{:S(2)}, u32[]{:S(2)}) collective-permute-start(bf16[128,256]{1,0:T(8,128)(2,1)S(1)} %convolution_convert_fusion), channel_id=1, source_target_pairs={{0,8},{1,9},{2,10},{3,11},{4,40},{5,41},{6,42},{7,43},{8,72},{9,73... | collective-permute-start | bytes 196616 | tf_op jit(solution)/shard_map/ppermute | solution.py:52
  15.4 5.1 %collective-permute-start.3 = (bf16[128,256]{1,0:T(8,128)(2,1)S(1)}, bf16[128,256]{1,0:T(8,128)(2,1)S(1)}, u32[]{:S(2)}, u32[]{:S(2)}) collective-permute-start(bf16[128,256]{1,0:T(8,128)(2,1)S(1)} %collective-permute-done), channel_id=1, source_target_pairs={{0,1},{1,0},{2,3},{3,2},{4,5},{5,4},{6,7},{7,6},{8,9},{9,8},{10,11... | collective-permute-start | bytes 196616 | tf_op jit(solution)/shard_map/ppermute | solution.py:52
  19.1 1.4 %collective-permute-start.4 = (bf16[128,256]{1,0:T(8,128)(2,1)S(1)}, bf16[128,256]{1,0:T(8,128)(2,1)S(1)}, u32[]{:S(2)}, u32[]{:S(2)}) collective-permute-start(bf16[128,256]{1,0:T(8,128)(2,1)S(1)} %collective-permute-done.1), channel_id=1, source_target_pairs={{0,1},{1,0},{2,3},{3,2},{4,5},{5,4},{6,7},{7,6},{8,9},{9,8},{10,11... | collective-permute-start | bytes 196616 | tf_op jit(solution)/shard_map/ppermute | solution.py:52
  20.4 15.2 %collective-permute-start.14 = (bf16[256,1536]{1,0:T(8,128)(2,1)S(1)}, bf16[256,1536]{1,0:T(8,128)(2,1)S(1)}, u32[]{:S(2)}, u32[]{:S(2)}) collective-permute-start(bf16[256,1536]{1,0:T(8,128)(2,1)S(1)} %broadcast_select_fusion.h0), channel_id=1, source_target_pairs={{0,32},{1,97},{2,34},{3,99},{4,36},{5,101},{6,38},{7,103},{8,40},{... | collective-permute-start | bytes 2359304 | tf_op jit(solution)/shard_map/ppermute | solution.py:52
  20.6 5.2 %collective-permute-start.5 = (bf16[2,128,256]{2,1,0:T(8,128)(2,1)S(1)}, bf16[2,128,256]{2,1,0:T(8,128)(2,1)S(1)}, u32[]{:S(2)}, u32[]{:S(2)}) collective-permute-start(bf16[2,128,256]{2,1,0:T(8,128)(2,1)S(1)} %pad_maximum_fusion), channel_id=1, source_target_pairs={{0,2},{1,15},{2,4},{3,1},{4,6},{5,3},{6,8},{7,5},{8,10},{9,7},{10,... | collective-permute-start | bytes 393224 | tf_op jit(solution)/shard_map/ppermute | solution.py:52
  22.9 7.8 %collective-permute-start.7 = (bf16[2,128,256]{2,1,0:T(8,128)(2,1)S(1)}, bf16[2,128,256]{2,1,0:T(8,128)(2,1)S(1)}, u32[]{:S(2)}, u32[]{:S(2)}) collective-permute-start(bf16[2,128,256]{2,1,0:T(8,128)(2,1)S(1)} %pad_maximum_fusion), channel_id=1, source_target_pairs={{0,14},{1,3},{2,0},{3,5},{4,2},{5,7},{6,4},{7,9},{8,6},{9,11},{10,... | collective-permute-start | bytes 393224 | tf_op jit(solution)/shard_map/ppermute | solution.py:52
  22.9 9.5 %collective-permute-start.8 = (bf16[2,128,256]{2,1,0:T(8,128)(2,1)S(1)}, bf16[2,128,256]{2,1,0:T(8,128)(2,1)S(1)}, u32[]{:S(2)}, u32[]{:S(2)}) collective-permute-start(bf16[2,128,256]{2,1,0:T(8,128)(2,1)S(1)} %pad_maximum_fusion), channel_id=1, source_target_pairs={{0,4},{1,13},{2,6},{3,15},{4,8},{5,1},{6,10},{7,3},{8,12},{9,5},{1... | collective-permute-start | bytes 393224 | tf_op jit(solution)/shard_map/ppermute | solution.py:52
  25.8 26.4 %collective-permute-start.6 = (bf16[256,1536]{1,0:T(8,128)(2,1)S(1)}, bf16[256,1536]{1,0:T(8,128)(2,1)S(1)}, u32[]{:S(2)}, u32[]{:S(2)}) collective-permute-start(bf16[256,1536]{1,0:T(8,128)(2,1)S(1)} %broadcast_select_fusion.h0), channel_id=1, source_target_pairs={{0,96},{1,33},{2,98},{3,35},{4,100},{5,37},{6,102},{7,39},{8,104},... | collective-permute-start | bytes 2359304 | tf_op jit(solution)/shard_map/ppermute | solution.py:52
  35.6 17.1 %collective-permute-start.18 = (bf16[256,1536]{1,0:T(8,128)(2,1)S(1)}, bf16[256,1536]{1,0:T(8,128)(2,1)S(1)}, u32[]{:S(2)}, u32[]{:S(2)}) collective-permute-start(bf16[256,1536]{1,0:T(8,128)(2,1)S(1)} %collective-permute-done.14.h1), channel_id=1, source_target_pairs={{0,32},{1,97},{2,34},{3,99},{4,36},{5,101},{6,38},{7,103},{8,40},{... | collective-permute-start | bytes 2359304 | tf_op jit(solution)/shard_map/ppermute | solution.py:52
  40.3 11.8 %collective-permute-start.10 = (bf16[8,128,256]{2,1,0:T(8,128)(2,1)S(1)}, bf16[8,128,256]{2,1,0:T(8,128)(2,1)S(1)}, u32[]{:S(2)}, u32[]{:S(2)}) collective-permute-start(bf16[8,128,256]{2,1,0:T(8,128)(2,1)S(1)} %constant_dynamic-update-slice_fusion.rest_0_), channel_id=1, source_target_pairs={{0,144},{1,17},{2,146},{3,19},{4,148},{5,21},{6,150},{7,23},{8,152... | collective-permute-start | bytes 1572872 | tf_op jit(solution)/shard_map/ppermute | solution.py:52
  40.3 11.8 %collective-permute-start.9 = (bf16[8,128,256]{2,1,0:T(8,128)(2,1)S(1)}, bf16[8,128,256]{2,1,0:T(8,128)(2,1)S(1)}, u32[]{:S(2)}, u32[]{:S(2)}) collective-permute-start(bf16[8,128,256]{2,1,0:T(8,128)(2,1)S(1)} %constant_dynamic-update-slice_fusion.rest_0_), channel_id=1, source_target_pairs={{0,16},{1,145},{2,18},{3,147},{4,20},{5,149},{6,22},{7,151},{8,24}... | collective-permute-start | bytes 1572872 | tf_op jit(solution)/shard_map/ppermute | solution.py:52
  42.4 1.7 %collective-permute-start.11 = (bf16[1536,128]{1,0:T(8,128)(2,1)S(1)}, bf16[1536,128]{1,0:T(8,128)(2,1)S(1)}, u32[]{:S(2)}, u32[]{:S(2)}) collective-permute-start(bf16[1536,128]{1,0:T(8,128)(2,1)S(1)} %copy-done), channel_id=1, source_target_pairs={{0,1},{1,0},{2,3},{3,2},{4,5},{5,4},{6,7},{7,6},{8,9},{9,8},{10,11... | collective-permute-start | bytes 1179656 | tf_op jit(solution)/shard_map/ppermute | solution.py:52
  44.1 10.6 %collective-permute-start.15 = (bf16[256,1536]{1,0:T(8,128)(2,1)S(1)}, bf16[256,1536]{1,0:T(8,128)(2,1)S(1)}, u32[]{:S(2)}, u32[]{:S(2)}) collective-permute-start(bf16[256,1536]{1,0:T(8,128)(2,1)S(1)} %broadcast_select_fusion.h0), channel_id=1, source_target_pairs={{0,1},{1,0},{2,3},{3,2},{4,5},{5,4},{6,7},{7,6},{8,9},{9,8},{10,11... | collective-permute-start | bytes 2359304 | tf_op jit(solution)/shard_map/ppermute | solution.py:52
  52.2 4.3 %collective-permute-start.16 = (bf16[256,1536]{1,0:T(8,128)(2,1)S(1)}, bf16[256,1536]{1,0:T(8,128)(2,1)S(1)}, u32[]{:S(2)}, u32[]{:S(2)}) collective-permute-start(bf16[256,1536]{1,0:T(8,128)(2,1)S(1)} %collective-permute-done.14.h1), channel_id=1, source_target_pairs={{0,1},{1,0},{2,3},{3,2},{4,5},{5,4},{6,7},{7,6},{8,9},{9,8},{10,11... | collective-permute-start | bytes 2359304 | tf_op jit(solution)/shard_map/ppermute | solution.py:52
  52.2 4.2 %collective-permute-start.17 = (bf16[256,1536]{1,0:T(8,128)(2,1)S(1)}, bf16[256,1536]{1,0:T(8,128)(2,1)S(1)}, u32[]{:S(2)}, u32[]{:S(2)}) collective-permute-start(bf16[256,1536]{1,0:T(8,128)(2,1)S(1)} %collective-permute-done.6.h2), channel_id=1, source_target_pairs={{0,1},{1,0},{2,3},{3,2},{4,5},{5,4},{6,7},{7,6},{8,9},{9,8},{10,11... | collective-permute-start | bytes 2359304 | tf_op jit(solution)/shard_map/ppermute | solution.py:52
  52.7 9.3 %collective-permute-start.19 = (bf16[256,1536]{1,0:T(8,128)(2,1)S(1)}, bf16[256,1536]{1,0:T(8,128)(2,1)S(1)}, u32[]{:S(2)}, u32[]{:S(2)}) collective-permute-start(bf16[256,1536]{1,0:T(8,128)(2,1)S(1)} %collective-permute-done.18.h3), channel_id=1, source_target_pairs={{0,1},{1,0},{2,3},{3,2},{4,5},{5,4},{6,7},{7,6},{8,9},{9,8},{10,11... | collective-permute-start | bytes 2359304 | tf_op jit(solution)/shard_map/ppermute | solution.py:52
  52.8 8.0 %collective-permute-start.12 = (bf16[4,128,256]{2,1,0:T(8,128)(2,1)S(1)}, bf16[4,128,256]{2,1,0:T(8,128)(2,1)S(1)}, u32[]{:S(2)}, u32[]{:S(2)}) collective-permute-start(bf16[4,128,256]{2,1,0:T(8,128)(2,1)S(1)} %slice.26), channel_id=1, source_target_pairs={{0,16},{1,145},{2,18},{3,147},{4,20},{5,149},{6,22},{7,151},{8,24}... | collective-permute-start | bytes 786440 | tf_op jit(solution)/shard_map/ppermute | solution.py:52
  54.7 7.3 %collective-permute-start.13 = (bf16[4,128,256]{2,1,0:T(8,128)(2,1)S(1)}, bf16[4,128,256]{2,1,0:T(8,128)(2,1)S(1)}, u32[]{:S(2)}, u32[]{:S(2)}) collective-permute-start(bf16[4,128,256]{2,1,0:T(8,128)(2,1)S(1)} %slice.27), channel_id=1, source_target_pairs={{0,144},{1,17},{2,146},{3,19},{4,148},{5,21},{6,150},{7,23},{8,152... | collective-permute-start | bytes 786440 | tf_op jit(solution)/shard_map/ppermute | solution.py:52

commit v6 on v4

--- a/solution.py
+++ b/solution.py
@@ -166,7 +166,7 @@
     z1, z2, z3 = (send(block, z_step(d)) for d in (1, -1, 2))
     ring = jnp.concatenate([block, z1, z2, z3])
 
-    h1, h2 = send(h0, x_step(1)), send(lax.optimization_barrier((h0, z1))[0], x_step(-1))
+    h1, h2 = send(h0, x_step(1)), send(lax.optimization_barrier((h0, z1, z2))[0], x_step(-1))
     y1, y2 = send(ring, y_step(1)), send(ring, y_step(-1))
     h3 = send(lax.optimization_barrier((h1, ring))[0], x_step(1))
     h2, y1, y2, cspair = lax.optimization_barrier((h2, y1, y2, cspair))

time: 84.1 us -> 86.5 us (1.029)
  blocking collectives: 19.2 us -> 22 us
  waiting for transfers between devices: 22 us -> 19.9 us
  starting transfers between devices: 35.4 us -> 37.1 us
    all_to_all x1, blocking collectives: 19.2 us -> 22 us  [on_device(): parts = lax.all_to_all(part.reshape(32, 16, 128), ('yh', 'yl', 'z'), 0, 0)]
    ppermute x20, waiting for transfers between devices: 22 us -> 19.9 us  [send(): return lax.ppermute(a, AXES, perm)]
    ppermute x20, starting transfers between devices: 35.4 us -> 37.1 us  [send(): return lax.ppermute(a, AXES, perm)]
  transfers between devices with their start and end apart: 20 -> 20, of which waited for: 9 -> 10; matrix products, arithmetic and copies ran while one was open for 1% -> 1% of each run, Pallas kernels for 3% -> 3%
where the time goes in v6:
time: 86.5 us; the launch traced here: 86.2 us
  starting transfers between devices  37.1 us (43%)
  blocking collectives  22 us (25%)
  waiting for transfers between devices  19.9 us (23%)
  Pallas kernels  5.35 us (6%)
  matrix products  1.05 us (1%)
    ppermute x20, starting transfers between devices, send(): return lax.ppermute(a, AXES, perm)  37.1 us
    all_to_all x1, blocking collectives, on_device(): parts = lax.all_to_all(part.reshape(32, 16, 128), ('yh', 'yl', 'z'), 0, 0)  22 us
    ppermute x20, waiting for transfers between devices, send(): return lax.ppermute(a, AXES, perm)  19.9 us
    pallas_call x2, Pallas kernels, call(): pl.pallas_call(kernel, out_shape=[jax.ShapeDtypeStruct(*shape) for shape...  5.35 us
  transfers between devices with their start and end apart: 20, of which 10 were waited for; matrix products, arithmetic and copies ran while one was open for 1% of the time, Pallas kernels for 3%

profile of v6, /device:TPU:32, one launch (start us, length us, event | category | flops | bytes accessed | tf_op | source)
XLA Modules:
  0.0 86.2 jit_solution(4031606022050649462)
XLA Ops:
  0.0 1.8 %collective-permute-start.2 = (bf16[256,1536]{1,0:T(8,128)(2,1)}, bf16[256,1536]{1,0:T(8,128)(2,1)S(1)}, u32[]{:S(2)}, u32[]{:S(2)}) collective-permute-start(bf16[256,1536]{1,0:T(8,128)(2,1)} %param.3), channel_id=1, source_target_pairs={{0,0},{1,128},{2,2},{3,130},{4,4},{5,132},{6,6},{7,134},{8,8},{9,1... | collective-permute-start | bytes 2359304 | tf_op jit(solution)/shard_map/ppermute | solution.py:52
  1.8 1.0 %convolution_convert_fusion = bf16[128,256]{1,0:T(8,128)(2,1)S(1)} fusion(bf16[256,1536]{1,0:T(8,128)(2,1)} %param.3, bf16[2,128,128]{2,1,0:T(8,128)(2,1)} %constant.15.clone, s32[]{:T(128)S(6)} %select_n.30), kind=kOutput, calls=%fused_computation | convolution fusion | flops 8421376 | bytes 163844 | tf_op jit(solution)/shard_map/dot_general | solution.py:157
  2.8 0.7 collective-permute-start
  3.5 9.7 %collective-permute-start.1 = (bf16[128,256]{1,0:T(8,128)(2,1)S(1)}, bf16[128,256]{1,0:T(8,128)(2,1)S(1)}, u32[]{:S(2)}, u32[]{:S(2)}) collective-permute-start(bf16[128,256]{1,0:T(8,128)(2,1)S(1)} %convolution_convert_fusion), channel_id=1, source_target_pairs={{0,8},{1,9},{2,10},{3,11},{4,40},{5,41},{6,42},{7,43},{8,72},{9,73... | collective-permute-start | bytes 196616 | tf_op jit(solution)/shard_map/ppermute | solution.py:52
  13.2 3.1 %collective-permute-done.1 = bf16[128,256]{1,0:T(8,128)(2,1)S(1)} collective-permute-done((bf16[128,256]{1,0:T(8,128)(2,1)S(1)}, bf16[128,256]{1,0:T(8,128)(2,1)S(1)}, u32[]{:S(2)}, u32[]{:S(2)}) %collective-permute-start.1) | collective-permute-done | bytes 65568 | tf_op jit(solution)/shard_map/ppermute | solution.py:52
  16.3 2.3 %collective-permute-start.3 = (bf16[128,256]{1,0:T(8,128)(2,1)S(1)}, bf16[128,256]{1,0:T(8,128)(2,1)S(1)}, u32[]{:S(2)}, u32[]{:S(2)}) collective-permute-start(bf16[128,256]{1,0:T(8,128)(2,1)S(1)} %collective-permute-done), channel_id=1, source_target_pairs={{0,1},{1,0},{2,3},{3,2},{4,5},{5,4},{6,7},{7,6},{8,9},{9,8},{10,11... | collective-permute-start | bytes 196616 | tf_op jit(solution)/shard_map/ppermute | solution.py:52
  18.7 0.1 collective-permute-start.4
  18.8 0.1 collective-permute-start.14
  18.8 0.7 collective-permute-done.3
  19.6 0.4 collective-permute-done.4
  20.0 1.6 %collective-permute-start.5 = (bf16[2,128,256]{2,1,0:T(8,128)(2,1)S(1)}, bf16[2,128,256]{2,1,0:T(8,128)(2,1)S(1)}, u32[]{:S(2)}, u32[]{:S(2)}) collective-permute-start(bf16[2,128,256]{2,1,0:T(8,128)(2,1)S(1)} %pad_maximum_fusion), channel_id=1, source_target_pairs={{0,2},{1,15},{2,4},{3,1},{4,6},{5,3},{6,8},{7,5},{8,10},{9,7},{10,... | collective-permute-start | bytes 393224 | tf_op jit(solution)/shard_map/ppermute | solution.py:52
  21.5 0.5 collective-permute-start.6
  22.1 3.9 %collective-permute-start.8 = (bf16[2,128,256]{2,1,0:T(8,128)(2,1)S(1)}, bf16[2,128,256]{2,1,0:T(8,128)(2,1)S(1)}, u32[]{:S(2)}, u32[]{:S(2)}) collective-permute-start(bf16[2,128,256]{2,1,0:T(8,128)(2,1)S(1)} %pad_maximum_fusion), channel_id=1, source_target_pairs={{0,4},{1,13},{2,6},{3,15},{4,8},{5,1},{6,10},{7,3},{8,12},{9,5},{1... | collective-permute-start | bytes 393224 | tf_op jit(solution)/shard_map/ppermute | solution.py:52
  26.0 0.5 collective-permute-done.6
  26.5 7.1 %collective-permute-start.7 = (bf16[256,1536]{1,0:T(8,128)(2,1)S(1)}, bf16[256,1536]{1,0:T(8,128)(2,1)S(1)}, u32[]{:S(2)}, u32[]{:S(2)}) collective-permute-start(bf16[256,1536]{1,0:T(8,128)(2,1)S(1)} %collective-permute-done.2.h0), channel_id=1, source_target_pairs={{0,96},{1,33},{2,98},{3,35},{4,100},{5,37},{6,102},{7,39},{8,104},... | collective-permute-start | bytes 2359304 | tf_op jit(solution)/shard_map/ppermute | solution.py:52
  33.7 1.9 %collective-permute-start.18 = (bf16[256,1536]{1,0:T(8,128)(2,1)S(1)}, bf16[256,1536]{1,0:T(8,128)(2,1)S(1)}, u32[]{:S(2)}, u32[]{:S(2)}) collective-permute-start(bf16[256,1536]{1,0:T(8,128)(2,1)S(1)} %collective-permute-done.14.h1), channel_id=1, source_target_pairs={{0,32},{1,97},{2,34},{3,99},{4,36},{5,101},{6,38},{7,103},{8,40},{... | collective-permute-start | bytes 2359304 | tf_op jit(solution)/shard_map/ppermute | solution.py:52
  35.6 2.3 %collective-permute-start.10 = (bf16[8,128,256]{2,1,0:T(8,128)(2,1)S(1)}, bf16[8,128,256]{2,1,0:T(8,128)(2,1)S(1)}, u32[]{:S(2)}, u32[]{:S(2)}) collective-permute-start(bf16[8,128,256]{2,1,0:T(8,128)(2,1)S(1)} %constant_dynamic-update-slice_fusion.rest_0_), channel_id=1, source_target_pairs={{0,144},{1,17},{2,146},{3,19},{4,148},{5,21},{6,150},{7,23},{8,152... | collective-permute-start | bytes 1572872 | tf_op jit(solution)/shard_map/ppermute | solution.py:52
  37.9 0.7 collective-permute-start.11
  38.6 1.6 %collective-permute-done.11.cspair = bf16[1536,128]{1,0:T(8,128)(2,1)S(1)} collective-permute-done((bf16[1536,128]{1,0:T(8,128)(2,1)}, bf16[1536,128]{1,0:T(8,128)(2,1)S(1)}, u32[]{:S(2)}, u32[]{:S(2)}) %collective-permute-start.11) | collective-permute-done | bytes 393248 | tf_op jit(solution)/shard_map/ppermute | solution.py:52
  40.1 0.4 collective-permute-start.15
  40.5 9.7 %collective-permute-done.10.rest_2_ = bf16[8,128,256]{2,1,0:T(8,128)(2,1)S(1)} collective-permute-done((bf16[8,128,256]{2,1,0:T(8,128)(2,1)S(1)}, bf16[8,128,256]{2,1,0:T(8,128)(2,1)S(1)}, u32[]{:S(2)}, u32[]{:S(2)}) %collective-permute-start.10) | collective-permute-done | bytes 524320 | tf_op jit(solution)/shard_map/ppermute | solution.py:52
  50.2 0.7 collective-permute-done.9.rest_1_
  51.0 0.2 collective-permute-done.18.h3
  51.2 0.5 collective-permute-start.19
  51.7 0.8 collective-permute-start.12
  52.5 2.8 %collective-permute-start.13 = (bf16[4,128,256]{2,1,0:T(8,128)(2,1)S(1)}, bf16[4,128,256]{2,1,0:T(8,128)(2,1)S(1)}, u32[]{:S(2)}, u32[]{:S(2)}) collective-permute-start(bf16[4,128,256]{2,1,0:T(8,128)(2,1)S(1)} %slice.27), channel_id=1, source_target_pairs={{0,144},{1,17},{2,146},{3,19},{4,148},{5,21},{6,150},{7,23},{8,152... | collective-permute-start | bytes 786440 | tf_op jit(solution)/shard_map/ppermute | solution.py:52
  55.3 2.5 %shard_map.37 = (f32[512,1536]{1,0:T(8,128)S(1)}, bf16[4,8,128,256]{3,2,1,0:T(8,128)(2,1)S(1)}) custom-call(bf16[256,1536]{1,0:T(8,128)(2,1)S(1)} %collective-permute-done.2.h0, bf16[256,1536]{1,0:T(8,128)(2,1)S(1)} %collective-permute-done.14.h1, bf16[256,1536]{1,0:T(8,128)(2,1)S(1)} %collective-permute-done.7.h2, ...), custom_call_target="tpu_custom_call" | custom-call | flops 1800000000 | bytes 9000000 | tf_op jit(solution)/shard_map/pallas_call | solution.py:142
  57.8 2.0 %collective-permute-done.12.y3 = bf16[4,128,256]{2,1,0:T(8,128)(2,1)S(1)} collective-permute-done((bf16[4,128,256]{2,1,0:T(8,128)(2,1)S(1)}, bf16[4,128,256]{2,1,0:T(8,128)(2,1)S(1)}, u32[]{:S(2)}, u32[]{:S(2)}) %collective-permute-start.12) | collective-permute-done | bytes 262176 | tf_op jit(solution)/shard_map/ppermute | solution.py:52
  59.8 0.9 %collective-permute-done.13.y4 = bf16[4,128,256]{2,1,0:T(8,128)(2,1)S(1)} collective-permute-done((bf16[4,128,256]{2,1,0:T(8,128)(2,1)S(1)}, bf16[4,128,256]{2,1,0:T(8,128)(2,1)S(1)}, u32[]{:S(2)}, u32[]{:S(2)}) %collective-permute-start.13) | collective-permute-done | bytes 262176 | tf_op jit(solution)/shard_map/ppermute | solution.py:52
  60.7 2.9 %shard_map.38 = f32[512,128]{1,0:T(8,128)S(1)} custom-call(f32[512,1536]{1,0:T(8,128)S(1)} %get-tuple-element.27.gram, bf16[4,8,128,256]{3,2,1,0:T(8,128)(2,1)S(1)} %get-tuple-element.28.blocks, bf16[256,1536]{1,0:T(8,128)(2,1)S(1)} %collective-permute-done.2.h0, bf16[256,1536]{1,0:T(8,128)(2,1)S(1)} %collective-permute-done.14.h1, ...), custom_call_target="tpu_custom_call" | custom-call | flops 1600000000 | bytes 9000000 | tf_op jit(solution)/shard_map/pallas_call | solution.py:142
  63.6 22.0 %all_to_all.5 = f32[32,16,128]{2,1,0:T(8,128)S(1)} all-to-all(f32[32,16,128]{2,1,0:T(8,128)S(1)} %bitcast.12), channel_id=1, replica_groups=mesh['yh'=2,'x'=4,'yl'=2,'z'=8,'c'=2] {'yh','yl','z'}, dimensions={0} | all-to-all | bytes 524288 | tf_op jit(solution)/shard_map/all_to_all | solution.py:184
  85.6 0.6 reduce_sum.9
  (26 shorter events, 0.2 us)
Async XLA Ops:
  0.0 16.3 %collective-permute-start.2 = (bf16[256,1536]{1,0:T(8,128)(2,1)}, bf16[256,1536]{1,0:T(8,128)(2,1)S(1)}, u32[]{:S(2)}, u32[]{:S(2)}) collective-permute-start(bf16[256,1536]{1,0:T(8,128)(2,1)} %param.3), channel_id=1, source_target_pairs={{0,0},{1,128},{2,2},{3,130},{4,4},{5,132},{6,6},{7,134},{8,8},{9,1... | collective-permute-start | bytes 2359304 | tf_op jit(solution)/shard_map/ppermute | solution.py:52
  2.8 10.4 %collective-permute-start = (bf16[128,256]{1,0:T(8,128)(2,1)S(1)}, bf16[128,256]{1,0:T(8,128)(2,1)S(1)}, u32[]{:S(2)}, u32[]{:S(2)}) collective-permute-start(bf16[128,256]{1,0:T(8,128)(2,1)S(1)} %convolution_convert_fusion), channel_id=1, source_target_pairs={{0,0},{1,1},{2,2},{3,3},{4,32},{5,33},{6,34},{7,35},{8,64},{9,65},... | collective-permute-start | bytes 196616 | tf_op jit(solution)/shard_map/ppermute | solution.py:52
  3.5 12.8 %collective-permute-start.1 = (bf16[128,256]{1,0:T(8,128)(2,1)S(1)}, bf16[128,256]{1,0:T(8,128)(2,1)S(1)}, u32[]{:S(2)}, u32[]{:S(2)}) collective-permute-start(bf16[128,256]{1,0:T(8,128)(2,1)S(1)} %convolution_convert_fusion), channel_id=1, source_target_pairs={{0,8},{1,9},{2,10},{3,11},{4,40},{5,41},{6,42},{7,43},{8,72},{9,73... | collective-permute-start | bytes 196616 | tf_op jit(solution)/shard_map/ppermute | solution.py:52
  16.3 3.2 %collective-permute-start.3 = (bf16[128,256]{1,0:T(8,128)(2,1)S(1)}, bf16[128,256]{1,0:T(8,128)(2,1)S(1)}, u32[]{:S(2)}, u32[]{:S(2)}) collective-permute-start(bf16[128,256]{1,0:T(8,128)(2,1)S(1)} %collective-permute-done), channel_id=1, source_target_pairs={{0,1},{1,0},{2,3},{3,2},{4,5},{5,4},{6,7},{7,6},{8,9},{9,8},{10,11... | collective-permute-start | bytes 196616 | tf_op jit(solution)/shard_map/ppermute | solution.py:52
  18.7 1.3 %collective-permute-start.4 = (bf16[128,256]{1,0:T(8,128)(2,1)S(1)}, bf16[128,256]{1,0:T(8,128)(2,1)S(1)}, u32[]{:S(2)}, u32[]{:S(2)}) collective-permute-start(bf16[128,256]{1,0:T(8,128)(2,1)S(1)} %collective-permute-done.1), channel_id=1, source_target_pairs={{0,1},{1,0},{2,3},{3,2},{4,5},{5,4},{6,7},{7,6},{8,9},{9,8},{10,11... | collective-permute-start | bytes 196616 | tf_op jit(solution)/shard_map/ppermute | solution.py:52
  18.8 14.9 %collective-permute-start.14 = (bf16[256,1536]{1,0:T(8,128)(2,1)S(1)}, bf16[256,1536]{1,0:T(8,128)(2,1)S(1)}, u32[]{:S(2)}, u32[]{:S(2)}) collective-permute-start(bf16[256,1536]{1,0:T(8,128)(2,1)S(1)} %collective-permute-done.2.h0), channel_id=1, source_target_pairs={{0,32},{1,97},{2,34},{3,99},{4,36},{5,101},{6,38},{7,103},{8,40},{... | collective-permute-start | bytes 2359304 | tf_op jit(solution)/shard_map/ppermute | solution.py:52
  20.0 6.0 %collective-permute-start.5 = (bf16[2,128,256]{2,1,0:T(8,128)(2,1)S(1)}, bf16[2,128,256]{2,1,0:T(8,128)(2,1)S(1)}, u32[]{:S(2)}, u32[]{:S(2)}) collective-permute-start(bf16[2,128,256]{2,1,0:T(8,128)(2,1)S(1)} %pad_maximum_fusion), channel_id=1, source_target_pairs={{0,2},{1,15},{2,4},{3,1},{4,6},{5,3},{6,8},{7,5},{8,10},{9,7},{10,... | collective-permute-start | bytes 393224 | tf_op jit(solution)/shard_map/ppermute | solution.py:52
  21.5 5.0 %collective-permute-start.6 = (bf16[2,128,256]{2,1,0:T(8,128)(2,1)S(1)}, bf16[2,128,256]{2,1,0:T(8,128)(2,1)S(1)}, u32[]{:S(2)}, u32[]{:S(2)}) collective-permute-start(bf16[2,128,256]{2,1,0:T(8,128)(2,1)S(1)} %pad_maximum_fusion), channel_id=1, source_target_pairs={{0,14},{1,3},{2,0},{3,5},{4,2},{5,7},{6,4},{7,9},{8,6},{9,11},{10,... | collective-permute-start | bytes 393224 | tf_op jit(solution)/shard_map/ppermute | solution.py:52
  22.1 11.6 %collective-permute-start.8 = (bf16[2,128,256]{2,1,0:T(8,128)(2,1)S(1)}, bf16[2,128,256]{2,1,0:T(8,128)(2,1)S(1)}, u32[]{:S(2)}, u32[]{:S(2)}) collective-permute-start(bf16[2,128,256]{2,1,0:T(8,128)(2,1)S(1)} %pad_maximum_fusion), channel_id=1, source_target_pairs={{0,4},{1,13},{2,6},{3,15},{4,8},{5,1},{6,10},{7,3},{8,12},{9,5},{1... | collective-permute-start | bytes 393224 | tf_op jit(solution)/shard_map/ppermute | solution.py:52
  26.5 24.4 %collective-permute-start.7 = (bf16[256,1536]{1,0:T(8,128)(2,1)S(1)}, bf16[256,1536]{1,0:T(8,128)(2,1)S(1)}, u32[]{:S(2)}, u32[]{:S(2)}) collective-permute-start(bf16[256,1536]{1,0:T(8,128)(2,1)S(1)} %collective-permute-done.2.h0), channel_id=1, source_target_pairs={{0,96},{1,33},{2,98},{3,35},{4,100},{5,37},{6,102},{7,39},{8,104},... | collective-permute-start | bytes 2359304 | tf_op jit(solution)/shard_map/ppermute | solution.py:52
  33.7 17.5 %collective-permute-start.18 = (bf16[256,1536]{1,0:T(8,128)(2,1)S(1)}, bf16[256,1536]{1,0:T(8,128)(2,1)S(1)}, u32[]{:S(2)}, u32[]{:S(2)}) collective-permute-start(bf16[256,1536]{1,0:T(8,128)(2,1)S(1)} %collective-permute-done.14.h1), channel_id=1, source_target_pairs={{0,32},{1,97},{2,34},{3,99},{4,36},{5,101},{6,38},{7,103},{8,40},{... | collective-permute-start | bytes 2359304 | tf_op jit(solution)/shard_map/ppermute | solution.py:52
  35.6 14.7 %collective-permute-start.10 = (bf16[8,128,256]{2,1,0:T(8,128)(2,1)S(1)}, bf16[8,128,256]{2,1,0:T(8,128)(2,1)S(1)}, u32[]{:S(2)}, u32[]{:S(2)}) collective-permute-start(bf16[8,128,256]{2,1,0:T(8,128)(2,1)S(1)} %constant_dynamic-update-slice_fusion.rest_0_), channel_id=1, source_target_pairs={{0,144},{1,17},{2,146},{3,19},{4,148},{5,21},{6,150},{7,23},{8,152... | collective-permute-start | bytes 1572872 | tf_op jit(solution)/shard_map/ppermute | solution.py:52
  37.9 13.1 %collective-permute-start.9 = (bf16[8,128,256]{2,1,0:T(8,128)(2,1)S(1)}, bf16[8,128,256]{2,1,0:T(8,128)(2,1)S(1)}, u32[]{:S(2)}, u32[]{:S(2)}) collective-permute-start(bf16[8,128,256]{2,1,0:T(8,128)(2,1)S(1)} %constant_dynamic-update-slice_fusion.rest_0_), channel_id=1, source_target_pairs={{0,16},{1,145},{2,18},{3,147},{4,20},{5,149},{6,22},{7,151},{8,24}... | collective-permute-start | bytes 1572872 | tf_op jit(solution)/shard_map/ppermute | solution.py:52
  37.9 2.3 %collective-permute-start.11 = (bf16[1536,128]{1,0:T(8,128)(2,1)}, bf16[1536,128]{1,0:T(8,128)(2,1)S(1)}, u32[]{:S(2)}, u32[]{:S(2)}) collective-permute-start(bf16[1536,128]{1,0:T(8,128)(2,1)} %pair.1), channel_id=1, source_target_pairs={{0,1},{1,0},{2,3},{3,2},{4,5},{5,4},{6,7},{7,6},{8,9},{9,8},{10,11... | collective-permute-start | bytes 1179656 | tf_op jit(solution)/shard_map/ppermute | solution.py:52
  40.1 12.3 %collective-permute-start.15 = (bf16[256,1536]{1,0:T(8,128)(2,1)S(1)}, bf16[256,1536]{1,0:T(8,128)(2,1)S(1)}, u32[]{:S(2)}, u32[]{:S(2)}) collective-permute-start(bf16[256,1536]{1,0:T(8,128)(2,1)S(1)} %collective-permute-done.2.h0), channel_id=1, source_target_pairs={{0,1},{1,0},{2,3},{3,2},{4,5},{5,4},{6,7},{7,6},{8,9},{9,8},{10,11... | collective-permute-start | bytes 2359304 | tf_op jit(solution)/shard_map/ppermute | solution.py:52
  50.2 5.1 %collective-permute-start.16 = (bf16[256,1536]{1,0:T(8,128)(2,1)S(1)}, bf16[256,1536]{1,0:T(8,128)(2,1)S(1)}, u32[]{:S(2)}, u32[]{:S(2)}) collective-permute-start(bf16[256,1536]{1,0:T(8,128)(2,1)S(1)} %collective-permute-done.14.h1), channel_id=1, source_target_pairs={{0,1},{1,0},{2,3},{3,2},{4,5},{5,4},{6,7},{7,6},{8,9},{9,8},{10,11... | collective-permute-start | bytes 2359304 | tf_op jit(solution)/shard_map/ppermute | solution.py:52
  51.0 4.4 %collective-permute-start.17 = (bf16[256,1536]{1,0:T(8,128)(2,1)S(1)}, bf16[256,1536]{1,0:T(8,128)(2,1)S(1)}, u32[]{:S(2)}, u32[]{:S(2)}) collective-permute-start(bf16[256,1536]{1,0:T(8,128)(2,1)S(1)} %collective-permute-done.7.h2), channel_id=1, source_target_pairs={{0,1},{1,0},{2,3},{3,2},{4,5},{5,4},{6,7},{7,6},{8,9},{9,8},{10,11... | collective-permute-start | bytes 2359304 | tf_op jit(solution)/shard_map/ppermute | solution.py:52
  51.2 9.5 %collective-permute-start.19 = (bf16[256,1536]{1,0:T(8,128)(2,1)S(1)}, bf16[256,1536]{1,0:T(8,128)(2,1)S(1)}, u32[]{:S(2)}, u32[]{:S(2)}) collective-permute-start(bf16[256,1536]{1,0:T(8,128)(2,1)S(1)} %collective-permute-done.18.h3), channel_id=1, source_target_pairs={{0,1},{1,0},{2,3},{3,2},{4,5},{5,4},{6,7},{7,6},{8,9},{9,8},{10,11... | collective-permute-start | bytes 2359304 | tf_op jit(solution)/shard_map/ppermute | solution.py:52
  51.7 8.1 %collective-permute-start.12 = (bf16[4,128,256]{2,1,0:T(8,128)(2,1)S(1)}, bf16[4,128,256]{2,1,0:T(8,128)(2,1)S(1)}, u32[]{:S(2)}, u32[]{:S(2)}) collective-permute-start(bf16[4,128,256]{2,1,0:T(8,128)(2,1)S(1)} %slice.26), channel_id=1, source_target_pairs={{0,16},{1,145},{2,18},{3,147},{4,20},{5,149},{6,22},{7,151},{8,24}... | collective-permute-start | bytes 786440 | tf_op jit(solution)/shard_map/ppermute | solution.py:52
  52.5 8.3 %copy-start = (bf16[1536,128]{1,0:T(8,128)(2,1)S(1)}, bf16[1536,128]{1,0:T(8,128)(2,1)}, u32[]{:S(2)}) copy-start(bf16[1536,128]{1,0:T(8,128)(2,1)} %pair.1) | copy-start | bytes 1179652
  52.5 8.2 %collective-permute-start.13 = (bf16[4,128,256]{2,1,0:T(8,128)(2,1)S(1)}, bf16[4,128,256]{2,1,0:T(8,128)(2,1)S(1)}, u32[]{:S(2)}, u32[]{:S(2)}) collective-permute-start(bf16[4,128,256]{2,1,0:T(8,128)(2,1)S(1)} %slice.27), channel_id=1, source_target_pairs={{0,144},{1,17},{2,146},{3,19},{4,148},{5,21},{6,150},{7,23},{8,152... | collective-permute-start | bytes 786440 | tf_op jit(solution)/shard_map/ppermute | solution.py:52
